TPU v7x, 32 devices: a whole 2x2x4 slice. The times are simulated.
32 devices in a mesh: dp: 8 (over z, core), tensor: 4 (over y, x).
Axes of the slice: x: 2, y: 2, z: 4, core: 2. Of those that a mesh axis runs over, the one named last changes fastest.
Arguments:
- tokens: bfloat16 [16, 128, 8, 512], P('dp', 'tensor'), may hold values from -6 to 6
- cotangent: bfloat16 [16, 128, 8, 512], P('dp', 'tensor'), may hold values from -6 to 6
- block_task: int32 [16], P('dp'), may hold values from 0 to 1, as said below
- sample_len: int32 [16], P('dp'), may hold values from 1 to 128, as said below
- feature_len: int32 [16], P('dp'), may hold values from 1 to 8, as said below
- norm_gain: float32 [2, 3, 512], replicated, may hold values from 0.5 to 1.5
- norm_shift: float32 [2, 3, 512], replicated, may hold values from -2 to 2
- sample_qkv: bfloat16 [2, 512, 3, 512], P(None, None, None, 'tensor'), may hold values from -0.25 to 0.25
- sample_out: bfloat16 [2, 512, 512], P(None, 'tensor'), may hold values from -0.75 to 0.75
- feature_qkv: bfloat16 [2, 512, 3, 512], P(None, None, None, 'tensor'), may hold values from -0.25 to 0.25
- feature_out: bfloat16 [2, 512, 512], P(None, 'tensor'), may hold values from -0.5 to 0.5
- out_bias: float32 [2, 3, 512], replicated, may hold values from -2 to 2
- up_weight: bfloat16 [2, 512, 2048], P(None, None, 'tensor'), may hold values from -0.25 to 0.25
- up_bias: float32 [2, 2048], replicated, may hold values from -2 to 2
- down_weight: bfloat16 [2, 2048, 512], P(None, 'tensor'), may hold values from -0.125 to 0.125
Outputs:
- output: bfloat16 [16, 128, 8, 512], P('dp', 'tensor')
- tokens_grad: float32 [16, 128, 8, 512], P('dp', 'tensor')
- norm_gain_grad: float32 [2, 3, 512], replicated
- norm_shift_grad: float32 [2, 3, 512], replicated
- sample_qkv_grad: float32 [2, 512, 3, 512], P(None, 'dp', None, 'tensor')
- sample_out_grad: float32 [2, 512, 512], P(None, 'tensor', 'dp')
- feature_qkv_grad: float32 [2, 512, 3, 512], P(None, 'dp', None, 'tensor')
- feature_out_grad: float32 [2, 512, 512], P(None, 'tensor', 'dp')
- out_bias_grad: float32 [2, 3, 512], replicated
- up_weight_grad: float32 [2, 512, 2048], P(None, 'dp', 'tensor')
- up_bias_grad: float32 [2, 2048], replicated
- down_weight_grad: float32 [2, 2048, 512], P(None, 'tensor', 'dp')
Inputs may be any that keep to these rules, and one draw needn't show every extreme that they name: `block_task`: each data group is 2 consecutive blocks; within it tables are numbered from 0 in block order without gaps, and a table never leaves its group. `sample_len`: only a table's last block may be short, and a group's first block is always full. `feature_len`: equal for all blocks of one table.
All inputs are finite; a program needn't handle non-finite values.
Results may differ from a plain program's by a relative error of at most 0.029.
Values may be sent and summed in bfloat16 or wider, within the bound.
No kernel may reach another device: no remote copies, remote signals or barrier semaphores. Data moves between devices by JAX's collectives and lax.ppermute only.
A program may use at most 192 MiB of HBM per device.

v0:
```python
import jax
import jax.numpy as jnp
from jax import lax
from jax.sharding import PartitionSpec as P

HD = 64
FF = 2048
L = 2


epsilon = 1e-05
masked_score = -1e30


def layer_norm(hidden_in, gain_row, shift_row):
    centre = hidden_in - jnp.mean(hidden_in, axis=-1, keepdims=True)
    spread = jnp.mean(centre * centre, axis=-1, keepdims=True)
    return centre * lax.rsqrt(spread + epsilon) * gain_row + shift_row


def norm_back(hidden_in, gain_row, shift_row, incoming):
    unused, pull = jax.vjp(layer_norm, hidden_in, gain_row, shift_row)
    return pull(incoming)


def gelu_back(up_value, incoming):
    unused, pull = jax.vjp(jax.nn.gelu, up_value)
    return pull(incoming)[0]


def log_total(scores):
    row_top = jnp.max(scores, axis=-1, keepdims=True)
    return row_top + jnp.log(jnp.sum(jnp.exp(scores - row_top), axis=-1, keepdims=True))


def sample_keys(block_task, sample_len, sample_rows):
    row_task = jnp.repeat(block_task, sample_rows)
    row_live = (jnp.arange(sample_rows)[None, :] < sample_len[:, None]).reshape(-1)
    return (row_task[:, None] == row_task[None, :]) & row_live[None, :]


def feature_keys(feature_len, feat_slots, sample_rows):
    live = jnp.arange(feat_slots)[None, :] < feature_len[:, None]
    return jnp.repeat(live, sample_rows, axis=0)[:, None, None, :]


def project(gathered, weight):
    blocks, sample_rows, feat_slots, width = gathered.shape
    head_count = weight.shape[-1] // HD
    projected = jnp.einsum("bsfd,dcx->cbsfx", gathered, weight, preferred_element_type=jnp.float32)
    return projected.astype(jnp.bfloat16).reshape(
        3, blocks * sample_rows, feat_slots, head_count, HD
    )


def sample_forward(projected, key_mask):
    query_all, key_all, value_all = (projected[0], projected[1], projected[2])
    row_count = query_all.shape[0]
    block_rows = min(row_count, 512)
    score_scale = HD ** (-0.5)

    def one_block(offset):
        scores = (
            jnp.einsum("qfhe,kfhe->fhqk", query_all, key_all, preferred_element_type=jnp.float32)
            * score_scale
        )
        scores = jnp.where(key_mask, scores, masked_score)
        totals = log_total(scores)
        weights = jnp.exp(scores - totals).astype(jnp.bfloat16)
        mixed = jnp.einsum(
            "fhqk,kfhe->qfhe", weights, value_all, preferred_element_type=jnp.float32
        )
        return (mixed.astype(jnp.bfloat16), totals)

    offsets = jnp.arange(row_count // block_rows, dtype=jnp.int32) * block_rows
    mixed, totals = lax.map(one_block, offsets)
    return (mixed.reshape(row_count, query_all.shape[1], -1), totals)


def sample_backward(projected, totals, mixed_grad, key_mask):
    query_all, key_all, value_all = (projected[0], projected[1], projected[2])
    row_count = query_all.shape[0]
    block_rows = min(row_count, 512)
    score_scale = HD ** (-0.5)

    def one_block(carry, item):
        key_grad, value_grad = carry
        offset, totals_part = item
        scores = (
            jnp.einsum("qfhe,kfhe->fhqk", query_all, key_all, preferred_element_type=jnp.float32)
            * score_scale
        )
        scores = jnp.where(key_mask, scores, masked_score)
        weights = jnp.exp(scores - totals_part)
        value_grad = value_grad + jnp.einsum(
            "fhqk,qfhe->kfhe",
            weights.astype(jnp.bfloat16),
            mixed_grad,
            preferred_element_type=jnp.float32,
        )
        weight_grad = jnp.einsum(
            "qfhe,kfhe->fhqk", mixed_grad, value_all, preferred_element_type=jnp.float32
        )
        score_grad = weights * (
            weight_grad - jnp.sum(weights * weight_grad, axis=-1, keepdims=True)
        )
        score_low = score_grad.astype(jnp.bfloat16)
        query_grad = (
            jnp.einsum("fhqk,kfhe->qfhe", score_low, key_all, preferred_element_type=jnp.float32)
            * score_scale
        )
        key_grad = (
            key_grad
            + jnp.einsum(
                "fhqk,qfhe->kfhe", score_low, query_all, preferred_element_type=jnp.float32
            )
            * score_scale
        )
        return ((key_grad, value_grad), query_grad)

    offsets = jnp.arange(row_count // block_rows, dtype=jnp.int32) * block_rows
    empty = jnp.zeros(key_all.shape, jnp.float32)
    (key_grad, value_grad), query_grad = lax.scan(one_block, (empty, empty), (offsets, totals))
    query_grad = query_grad.reshape(key_all.shape)
    return jnp.stack([query_grad, key_grad, value_grad]).astype(jnp.bfloat16)


def feature_forward(projected, key_mask):
    query_all, key_all, value_all = (projected[0], projected[1], projected[2])
    scores = jnp.einsum(
        "qfhe,qghe->qhfg", query_all, key_all, preferred_element_type=jnp.float32
    ) * HD ** (-0.5)
    scores = jnp.where(key_mask, scores, masked_score)
    totals = log_total(scores)
    weights = jnp.exp(scores - totals).astype(jnp.bfloat16)
    mixed = jnp.einsum("qhfg,qghe->qfhe", weights, value_all, preferred_element_type=jnp.float32)
    return (mixed.astype(jnp.bfloat16).reshape(query_all.shape[0], query_all.shape[1], -1), totals)


def feature_backward(projected, totals, mixed_grad, key_mask):
    query_all, key_all, value_all = (projected[0], projected[1], projected[2])
    score_scale = HD ** (-0.5)
    scores = (
        jnp.einsum("qfhe,qghe->qhfg", query_all, key_all, preferred_element_type=jnp.float32)
        * score_scale
    )
    scores = jnp.where(key_mask, scores, masked_score)
    weights = jnp.exp(scores - totals)
    value_grad = jnp.einsum(
        "qhfg,qfhe->qghe",
        weights.astype(jnp.bfloat16),
        mixed_grad,
        preferred_element_type=jnp.float32,
    )
    weight_grad = jnp.einsum(
        "qfhe,qghe->qhfg", mixed_grad, value_all, preferred_element_type=jnp.float32
    )
    score_grad = weights * (weight_grad - jnp.sum(weights * weight_grad, axis=-1, keepdims=True))
    score_low = score_grad.astype(jnp.bfloat16)
    query_grad = (
        jnp.einsum("qhfg,qghe->qfhe", score_low, key_all, preferred_element_type=jnp.float32)
        * score_scale
    )
    key_grad = (
        jnp.einsum("qhfg,qfhe->qghe", score_low, query_all, preferred_element_type=jnp.float32)
        * score_scale
    )
    return jnp.stack([query_grad, key_grad, value_grad]).astype(jnp.bfloat16)


def attention_forward(state, gain_row, shift_row, weight, out_weight, out_shift, key_mask, attend):
    normed = layer_norm(state, gain_row, shift_row).astype(jnp.bfloat16)
    gathered = lax.all_gather(normed, "tensor", axis=1, tiled=True)
    projected = project(gathered, weight)
    mixed, totals = attend(projected, key_mask)
    partial_out = jnp.einsum("qfx,xd->qfd", mixed, out_weight, preferred_element_type=jnp.float32)
    branch = lax.psum_scatter(
        partial_out.reshape(gathered.shape).astype(jnp.bfloat16),
        "tensor",
        scatter_dimension=1,
        tiled=True,
    ).astype(jnp.float32)
    return (state + branch + out_shift, (state, gathered, projected, mixed, totals))


def attention_backward(
    state_grad, kept, gain_row, shift_row, weight, out_weight, key_mask, attend_back
):
    state_in, gathered, projected, mixed, totals = kept
    grad_low = state_grad.astype(jnp.bfloat16)
    bias_grad = jnp.sum(grad_low.astype(jnp.float32), axis=(0, 1, 2))
    grad_rows = lax.all_gather(grad_low, "tensor", axis=1, tiled=True)
    blocks, sample_rows, feat_slots, width = gathered.shape
    grad_flat = grad_rows.reshape(blocks * sample_rows, feat_slots, width)
    out_grad = jnp.einsum("qfx,qfd->xd", mixed, grad_flat, preferred_element_type=jnp.float32)
    mixed_grad = jnp.einsum(
        "qfd,xd->qfx", grad_flat, out_weight, preferred_element_type=jnp.float32
    )
    mixed_grad = mixed_grad.astype(jnp.bfloat16).reshape(projected.shape[1:])
    proj_grad = attend_back(projected, totals, mixed_grad, key_mask)
    proj_grad = proj_grad.reshape(3, blocks, sample_rows, feat_slots, -1)
    weight_grad = jnp.einsum(
        "bsfd,cbsfx->dcx", gathered, proj_grad, preferred_element_type=jnp.float32
    )
    normed_grad = jnp.einsum(
        "cbsfx,dcx->bsfd", proj_grad, weight, preferred_element_type=jnp.float32
    )
    normed_grad = lax.psum_scatter(
        normed_grad.astype(jnp.bfloat16), "tensor", scatter_dimension=1, tiled=True
    ).astype(jnp.float32)
    input_grad, gain_grad, norm_shift_grad = norm_back(state_in, gain_row, shift_row, normed_grad)
    return (state_grad + input_grad, (gain_grad, norm_shift_grad, bias_grad, weight_grad, out_grad))


def mlp_forward(state, gain_row, shift_row, up_part, up_shift, down_part, down_shift):
    normed = layer_norm(state, gain_row, shift_row).astype(jnp.bfloat16)
    rows_in = lax.all_gather(normed, "tensor", axis=1, tiled=True)
    hidden_count = up_part.shape[1]
    shift_part = lax.dynamic_slice_in_dim(
        up_shift, lax.axis_index("tensor") * hidden_count, hidden_count, 0
    )
    up_value = (
        jnp.einsum("bsfd,dk->bsfk", rows_in, up_part, preferred_element_type=jnp.float32)
        + shift_part
    )
    hidden = jax.nn.gelu(up_value).astype(jnp.bfloat16)
    partial_out = jnp.einsum("bsfk,kd->bsfd", hidden, down_part, preferred_element_type=jnp.float32)
    branch = lax.psum_scatter(
        partial_out.astype(jnp.bfloat16), "tensor", scatter_dimension=1, tiled=True
    ).astype(jnp.float32)
    up_used, down_used = (up_part, down_part)
    return (state + branch + down_shift, (state, rows_in, up_value, hidden, up_used, down_used))


def mlp_backward(state_grad, kept, gain_row, shift_row):
    state_in, rows_in, up_value, hidden, up_used, down_used = kept
    grad_low = state_grad.astype(jnp.bfloat16)
    bias_grad = jnp.sum(grad_low.astype(jnp.float32), axis=(0, 1, 2))
    grad_rows = lax.all_gather(grad_low, "tensor", axis=1, tiled=True)
    down_grad = jnp.einsum("bsfk,bsfd->kd", hidden, grad_rows, preferred_element_type=jnp.float32)
    hidden_grad = jnp.einsum(
        "bsfd,kd->bsfk", grad_rows, down_used, preferred_element_type=jnp.float32
    )
    up_grad = gelu_back(up_value, hidden_grad).astype(jnp.bfloat16)
    up_w_grad = jnp.einsum("bsfd,bsfk->dk", rows_in, up_grad, preferred_element_type=jnp.float32)
    up_b_grad = jnp.sum(up_grad.astype(jnp.float32), axis=(0, 1, 2))
    normed_grad = jnp.einsum("bsfk,dk->bsfd", up_grad, up_used, preferred_element_type=jnp.float32)
    normed_grad = lax.psum_scatter(
        normed_grad.astype(jnp.bfloat16), "tensor", scatter_dimension=1, tiled=True
    ).astype(jnp.float32)
    hidden_count = up_used.shape[1]
    up_b_grad = lax.dynamic_update_slice_in_dim(
        jnp.zeros((FF,), jnp.float32), up_b_grad, lax.axis_index("tensor") * hidden_count, 0
    )
    input_grad, gain_grad, norm_shift_grad = norm_back(state_in, gain_row, shift_row, normed_grad)
    return (
        state_grad + input_grad,
        (gain_grad, norm_shift_grad, bias_grad, up_w_grad, up_b_grad, down_grad),
    )


def body(
    tokens,
    cotangent,
    block_task,
    sample_len,
    feature_len,
    norm_gain,
    norm_shift,
    sample_qkv,
    sample_out,
    feature_qkv,
    feature_out,
    out_bias,
    up_weight,
    up_bias,
    down_weight,
):
    blocks, local_rows, feat_slots, width = tokens.shape
    sample_rows = local_rows * lax.axis_size("tensor")
    sample_mask = sample_keys(block_task, sample_len, sample_rows)
    feature_mask = feature_keys(feature_len, feat_slots, sample_rows)
    state = tokens.astype(jnp.float32)
    kept_all = []
    for layer_at in range(L):
        state, kept_sample = attention_forward(
            state,
            norm_gain[layer_at, 0],
            norm_shift[layer_at, 0],
            sample_qkv[layer_at],
            sample_out[layer_at],
            out_bias[layer_at, 0],
            sample_mask,
            sample_forward,
        )
        state, kept_feature = attention_forward(
            state,
            norm_gain[layer_at, 1],
            norm_shift[layer_at, 1],
            feature_qkv[layer_at],
            feature_out[layer_at],
            out_bias[layer_at, 1],
            feature_mask,
            feature_forward,
        )
        state, kept_mlp = mlp_forward(
            state,
            norm_gain[layer_at, 2],
            norm_shift[layer_at, 2],
            up_weight[layer_at],
            up_bias[layer_at],
            down_weight[layer_at],
            out_bias[layer_at, 2],
        )
        kept_all.append((kept_sample, kept_feature, kept_mlp))
    output = state.astype(jnp.bfloat16)
    sample_ids = lax.axis_index("tensor") * local_rows + jnp.arange(local_rows)
    sample_live = sample_ids[None, :] < sample_len[:, None]
    feature_live = jnp.arange(feat_slots)[None, :] < feature_len[:, None]
    live = (sample_live[:, :, None] & feature_live[:, None, :]).astype(jnp.float32)
    state_grad = cotangent.astype(jnp.float32) * live[..., None]
    small_terms = [None] * L
    weight_terms = [None] * L
    for layer_at in reversed(range(L)):
        kept_sample, kept_feature, kept_mlp = kept_all[layer_at]
        state_grad, mlp_terms = mlp_backward(
            state_grad, kept_mlp, norm_gain[layer_at, 2], norm_shift[layer_at, 2]
        )
        state_grad, feature_terms = attention_backward(
            state_grad,
            kept_feature,
            norm_gain[layer_at, 1],
            norm_shift[layer_at, 1],
            feature_qkv[layer_at],
            feature_out[layer_at],
            feature_mask,
            feature_backward,
        )
        state_grad, sample_terms = attention_backward(
            state_grad,
            kept_sample,
            norm_gain[layer_at, 0],
            norm_shift[layer_at, 0],
            sample_qkv[layer_at],
            sample_out[layer_at],
            sample_mask,
            sample_backward,
        )
        small_terms[layer_at] = (
            jnp.stack([sample_terms[0], feature_terms[0], mlp_terms[0]]),
            jnp.stack([sample_terms[1], feature_terms[1], mlp_terms[1]]),
            jnp.stack([sample_terms[2], feature_terms[2], mlp_terms[2]]),
            mlp_terms[4],
        )
        layer_weights = (
            sample_terms[3],
            sample_terms[4],
            feature_terms[3],
            feature_terms[4],
            mlp_terms[3],
            mlp_terms[5],
        )
        weight_terms[layer_at] = layer_weights
    stacked = tuple(
        (
            jnp.stack([weight_terms[layer_at][member] for layer_at in range(L)])
            for member in range(6)
        )
    )
    stacked = (
        lax.psum_scatter(
            stacked[0].astype(jnp.bfloat16), "dp", scatter_dimension=1, tiled=True
        ).astype(jnp.float32),
        lax.psum_scatter(
            stacked[1].astype(jnp.bfloat16), "dp", scatter_dimension=2, tiled=True
        ).astype(jnp.float32),
        lax.psum_scatter(
            stacked[2].astype(jnp.bfloat16), "dp", scatter_dimension=1, tiled=True
        ).astype(jnp.float32),
        lax.psum_scatter(
            stacked[3].astype(jnp.bfloat16), "dp", scatter_dimension=2, tiled=True
        ).astype(jnp.float32),
        lax.psum_scatter(
            stacked[4].astype(jnp.bfloat16), "dp", scatter_dimension=1, tiled=True
        ).astype(jnp.float32),
        lax.psum_scatter(
            stacked[5].astype(jnp.bfloat16), "dp", scatter_dimension=2, tiled=True
        ).astype(jnp.float32),
    )
    small_stacked = tuple(
        (jnp.stack([small_terms[layer_at][member] for layer_at in range(L)]) for member in range(4))
    )
    gain_total, shift_total, bias_total, up_bias_total = lax.psum(small_stacked, ("dp", "tensor"))
    return (
        output,
        state_grad,
        gain_total,
        shift_total,
        stacked[0],
        stacked[1],
        stacked[2],
        stacked[3],
        bias_total,
        stacked[4],
        up_bias_total,
        stacked[5],
    )


def solution(mesh):
    placed = (
        P("dp", "tensor", None, None),
        P("dp", "tensor", None, None),
        P("dp"),
        P("dp"),
        P("dp"),
        P(),
        P(),
        P(None, None, None, "tensor"),
        P(None, "tensor", None),
        P(None, None, None, "tensor"),
        P(None, "tensor", None),
        P(),
        P(None, None, "tensor"),
        P(),
        P(None, "tensor", None),
    )
    return jax.shard_map(
        body,
        mesh=mesh,
        in_specs=placed,
        out_specs=(
            P("dp", "tensor", None, None),
            P("dp", "tensor", None, None),
            P(),
            P(),
            P(None, "dp", None, "tensor"),
            P(None, "tensor", "dp"),
            P(None, "dp", None, "tensor"),
            P(None, "tensor", "dp"),
            P(),
            P(None, "dp", "tensor"),
            P(),
            P(None, "tensor", "dp"),
        ),
        check_vma=False,
    )
```

profile of v0, /device:TPU:0, one launch (start us, length us, event | category | flops | bytes accessed | tf_op | source)
XLA Modules:
  0.0 1385.9 jit_solution(14648250486102784780)
XLA Ops:
  15.3 37.8 %all-gather.13.cloned.1.call-done = bf16[2,128,8,512]{3,1,2,0:T(8,128)(2,1)} async-done(((bf16[2,32,8,512]{3,1,2,0:T(8,128)(2,1)}), bf16[2,128,8,512]{3,1,2,0:T(8,128)(2,1)}) %all-gather.13.cloned.1.call-update) | async-done | bytes 2097168 | tf_op jit(solution)/shard_map/all_gather | solution.py:173
  66.2 34.7 %reduce-scatter.16.cloned.1.call-done = bf16[2,32,8,512]{3,1,2,0:T(8,128)(2,1)} async-done(((bf16[2,128,8,512]{3,1,2,0:T(8,128)(2,1)}), bf16[2,32,8,512]{3,1,2,0:T(8,128)(2,1)}) %reduce-scatter.16.cloned.1.call-update) | async-done | bytes 524304 | tf_op jit(solution)/shard_map/reduce_scatter | solution.py:177
  105.4 35.1 %all-gather.15.cloned.1.call-done = bf16[2,128,8,512]{3,1,2,0:T(8,128)(2,1)} async-done(((bf16[2,32,8,512]{3,1,2,0:T(8,128)(2,1)}), bf16[2,128,8,512]{3,1,2,0:T(8,128)(2,1)}) %all-gather.15.cloned.1.call-update) | async-done | bytes 2097168 | tf_op jit(solution)/shard_map/all_gather | solution.py:173
  165.2 35.3 %reduce-scatter.18.cloned.1.call-done = bf16[2,32,8,512]{3,1,2,0:T(8,128)(2,1)} async-done(((bf16[2,128,8,512]{3,1,2,0:T(8,128)(2,1)}), bf16[2,32,8,512]{3,1,2,0:T(8,128)(2,1)}) %reduce-scatter.18.cloned.1.call-update) | async-done | bytes 524304 | tf_op jit(solution)/shard_map/reduce_scatter | solution.py:177
  205.9 33.6 %all-gather.17.cloned.1.call-done = bf16[2,128,8,512]{3,1,2,0:T(8,128)(2,1)} async-done(((bf16[2,32,8,512]{3,1,2,0:T(8,128)(2,1)}), bf16[2,128,8,512]{3,1,2,0:T(8,128)(2,1)}) %all-gather.17.cloned.1.call-update) | async-done | bytes 2097168 | tf_op jit(solution)/shard_map/all_gather | solution.py:217
  247.7 35.3 %reduce-scatter.20.cloned.1.call-done = bf16[2,32,8,512]{3,1,2,0:T(8,128)(2,1)} async-done(((bf16[2,128,8,512]{3,1,2,0:T(8,128)(2,1)}), bf16[2,32,8,512]{3,1,2,0:T(8,128)(2,1)}) %reduce-scatter.20.cloned.1.call-update) | async-done | bytes 524304 | tf_op jit(solution)/shard_map/reduce_scatter | solution.py:228
  287.4 35.4 %all-gather.19.cloned.1.call-done = bf16[2,128,8,512]{3,1,2,0:T(8,128)(2,1)} async-done(((bf16[2,32,8,512]{3,1,2,0:T(8,128)(2,1)}), bf16[2,128,8,512]{3,1,2,0:T(8,128)(2,1)}) %all-gather.19.cloned.1.call-update) | async-done | bytes 2097168 | tf_op jit(solution)/shard_map/all_gather | solution.py:173
  350.5 35.3 %reduce-scatter.22.cloned.1.call-done = bf16[2,32,8,512]{3,1,2,0:T(8,128)(2,1)} async-done(((bf16[2,128,8,512]{3,1,2,0:T(8,128)(2,1)}), bf16[2,32,8,512]{3,1,2,0:T(8,128)(2,1)}) %reduce-scatter.22.cloned.1.call-update) | async-done | bytes 524304 | tf_op jit(solution)/shard_map/reduce_scatter | solution.py:177
  390.3 35.2 %all-gather.21.cloned.1.call-done = bf16[2,128,8,512]{3,1,2,0:T(8,128)(2,1)} async-done(((bf16[2,32,8,512]{3,1,2,0:T(8,128)(2,1)}), bf16[2,128,8,512]{3,1,2,0:T(8,128)(2,1)}) %all-gather.21.cloned.1.call-update) | async-done | bytes 2097168 | tf_op jit(solution)/shard_map/all_gather | solution.py:173
  465.5 35.3 %reduce-scatter.24.cloned.1.call-done = bf16[2,32,8,512]{3,1,2,0:T(8,128)(2,1)} async-done(((bf16[2,128,8,512]{3,1,2,0:T(8,128)(2,1)}), bf16[2,32,8,512]{3,1,2,0:T(8,128)(2,1)}) %reduce-scatter.24.cloned.1.call-update) | async-done | bytes 524304 | tf_op jit(solution)/shard_map/reduce_scatter | solution.py:177
  508.8 31.0 %all-gather.23.cloned.1.call-done = bf16[2,128,8,512]{3,1,2,0:T(8,128)(2,1)} async-done(((bf16[2,32,8,512]{3,1,2,0:T(8,128)(2,1)}), bf16[2,128,8,512]{3,1,2,0:T(8,128)(2,1)}) %all-gather.23.cloned.1.call-update) | async-done | bytes 2097168 | tf_op jit(solution)/shard_map/all_gather | solution.py:217
  539.8 5.0 fusion.229
  544.9 32.2 %all-gather.25.cloned.1.call-done = bf16[2,128,8,512]{3,1,2,0:T(8,128)(2,1)} async-done(((bf16[2,32,8,512]{3,1,2,0:T(8,128)(2,1)}), bf16[2,128,8,512]{3,1,2,0:T(8,128)(2,1)}) %all-gather.25.cloned.1.call-update) | async-done | bytes 2097168 | tf_op jit(solution)/shard_map/all_gather | solution.py:239
  577.0 7.5 convert_reduce_fusion
  588.5 35.3 %reduce-scatter.28.cloned.1.call-done = bf16[2,32,8,512]{3,1,2,0:T(8,128)(2,1)} async-done(((bf16[2,128,8,512]{3,1,2,0:T(8,128)(2,1)}), bf16[2,32,8,512]{3,1,2,0:T(8,128)(2,1)}) %reduce-scatter.28.cloned.1.call-update) | async-done | bytes 524304 | tf_op jit(solution)/shard_map/reduce_scatter | solution.py:248
  631.6 35.0 %all-gather.27.cloned.1.call-done = bf16[2,128,8,512]{3,1,2,0:T(8,128)(2,1)} async-done(((bf16[2,32,8,512]{3,1,2,0:T(8,128)(2,1)}), bf16[2,128,8,512]{3,1,2,0:T(8,128)(2,1)}) %all-gather.27.cloned.1.call-update) | async-done | bytes 2097168 | tf_op jit(solution)/shard_map/all_gather | solution.py:192
  710.4 5.4 convolution_convert_fusion.6
  715.9 29.3 %reduce-scatter.30.cloned.1.call-done = bf16[2,32,8,512]{3,1,2,0:T(8,128)(2,1)} async-done(((bf16[2,128,8,512]{3,1,2,0:T(8,128)(2,1)}), bf16[2,32,8,512]{3,1,2,0:T(8,128)(2,1)}) %reduce-scatter.30.cloned.1.call-update) | async-done | bytes 524304 | tf_op jit(solution)/shard_map/reduce_scatter | solution.py:208
  751.1 32.3 %reduce-scatter.26.cloned.1.call-done = bf16[2,32,8,512]{3,1,2,0:T(8,128)(2,1)} async-done(((bf16[2,128,8,512]{3,1,2,0:T(8,128)(2,1)}), bf16[2,32,8,512]{3,1,2,0:T(8,128)(2,1)}) %reduce-scatter.26.cloned.1.call-update) | async-done | bytes 524304 | tf_op jit(solution)/shard_map/reduce_scatter | solution.py:228
  787.9 35.4 %all-gather.29.cloned.1.call-done = bf16[2,128,8,512]{3,1,2,0:T(8,128)(2,1)} async-done(((bf16[2,32,8,512]{3,1,2,0:T(8,128)(2,1)}), bf16[2,128,8,512]{3,1,2,0:T(8,128)(2,1)}) %all-gather.29.cloned.1.call-update) | async-done | bytes 2097168 | tf_op jit(solution)/shard_map/all_gather | solution.py:192
  851.9 35.1 %reduce-scatter.32.cloned.1.call-done = bf16[2,32,8,512]{3,1,2,0:T(8,128)(2,1)} async-done(((bf16[2,128,8,512]{3,1,2,0:T(8,128)(2,1)}), bf16[2,32,8,512]{3,1,2,0:T(8,128)(2,1)}) %reduce-scatter.32.cloned.1.call-update) | async-done | bytes 524304 | tf_op jit(solution)/shard_map/reduce_scatter | solution.py:208
  893.7 35.4 %all-gather.31.cloned.1.call-done = bf16[2,128,8,512]{3,1,2,0:T(8,128)(2,1)} async-done(((bf16[2,32,8,512]{3,1,2,0:T(8,128)(2,1)}), bf16[2,128,8,512]{3,1,2,0:T(8,128)(2,1)}) %all-gather.31.cloned.1.call-update) | async-done | bytes 2097168 | tf_op jit(solution)/shard_map/all_gather | solution.py:239
  929.1 7.5 convert_reduce_fusion.1
  940.6 35.3 %reduce-scatter.34.cloned.1.call-done = bf16[2,32,8,512]{3,1,2,0:T(8,128)(2,1)} async-done(((bf16[2,128,8,512]{3,1,2,0:T(8,128)(2,1)}), bf16[2,32,8,512]{3,1,2,0:T(8,128)(2,1)}) %reduce-scatter.34.cloned.1.call-update) | async-done | bytes 524304 | tf_op jit(solution)/shard_map/reduce_scatter | solution.py:248
  984.9 35.0 %all-gather.33.cloned.1.call-done = bf16[2,128,8,512]{3,1,2,0:T(8,128)(2,1)} async-done(((bf16[2,32,8,512]{3,1,2,0:T(8,128)(2,1)}), bf16[2,128,8,512]{3,1,2,0:T(8,128)(2,1)}) %all-gather.33.cloned.1.call-update) | async-done | bytes 2097168 | tf_op jit(solution)/shard_map/all_gather | solution.py:192
  1052.6 35.1 %reduce-scatter.36.cloned.1.call-done = bf16[2,32,8,512]{3,1,2,0:T(8,128)(2,1)} async-done(((bf16[2,128,8,512]{3,1,2,0:T(8,128)(2,1)}), bf16[2,32,8,512]{3,1,2,0:T(8,128)(2,1)}) %reduce-scatter.36.cloned.1.call-update) | async-done | bytes 524304 | tf_op jit(solution)/shard_map/reduce_scatter | solution.py:208
  1098.2 4.4 fusion.149
  1168.9 27.8 %reduce-scatter.42.cloned.1.call-done = bf16[2,64,3,128]{3,1,2,0:T(8,128)(2,1)} async-done(((bf16[2,512,3,128]{3,1,2,0:T(8,128)(2,1)}), bf16[2,64,3,128]{3,1,2,0:T(8,128)(2,1)}) %reduce-scatter.42.cloned.1.call-update) | async-done | bytes 98320 | tf_op jit(solution)/shard_map/reduce_scatter | solution.py:377
  1198.4 62.3 %all-reduce.7.cloned.1.call-done = (bf16[2,128,512]{1,0,2:T(2,128)(2,1)}, bf16[2,128,512]{1,0,2:T(2,128)(2,1)}, bf16[2,512,512]{1,0,2:T(2,128)(2,1)}) async-done(((bf16[2,128,512]{1,0,2:T(2,128)(2,1)}, bf16[2,128,512]{1,0,2:T(2,128)(2,1)}, bf16[2,512,512]{1,0,2:T(2,128)(2,1)}), (bf16[2,128,512]{1,0,2:T(2,128)(2,1)}, bf16[2,128,512]{1,0,2:T(2,128)(2,1)}, ...) | async-done | bytes 1572880
  1264.5 29.4 %reduce-scatter.40.cloned.1.call-done = bf16[2,64,3,128]{3,1,2,0:T(8,128)(2,1)} async-done(((bf16[2,512,3,128]{3,1,2,0:T(8,128)(2,1)}), bf16[2,64,3,128]{3,1,2,0:T(8,128)(2,1)}) %reduce-scatter.40.cloned.1.call-update) | async-done | bytes 98320 | tf_op jit(solution)/shard_map/reduce_scatter | solution.py:371
  1295.5 35.0 %reduce-scatter.38.cloned.1.call-done = bf16[2,32,8,512]{3,1,2,0:T(8,128)(2,1)} async-done(((bf16[2,128,8,512]{3,1,2,0:T(8,128)(2,1)}), bf16[2,32,8,512]{3,1,2,0:T(8,128)(2,1)}) %reduce-scatter.38.cloned.1.call-update) | async-done | bytes 524304 | tf_op jit(solution)/shard_map/reduce_scatter | solution.py:208
  1334.1 40.1 %all-reduce.3 = (f32[2,3,512]{2,1,0:T(4,128)S(1)}, f32[2,3,512]{2,1,0:T(4,128)S(1)}, f32[2,3,512]{2,1,0:T(4,128)S(1)}, f32[2,2048]{1,0:T(2,128)}) all-reduce(f32[2,3,512]{2,1,0:T(4,128)S(1)} %pad_maximum_fusion.18, f32[2,3,512]{2,1,0:T(4,128)S(1)} %pad_maximum_fusion.19, ...), channel_id=1, replica_groups=mesh['dp'=8,'tensor'=4] {'dp','tensor'}, use_global_device_ids=true, to_apply=%region_54.55 | all-reduce | flops 13312 | bytes 106496 | tf_op jit(solution)/shard_map/psum | solution.py:393
  (648 shorter events, 384.4 us)
Async XLA Ops:
  7.2 45.9 %all-gather.13.cloned.1.call-start = ((), (), s32[]{:S(2)}) async-start(), calls=%async_computation.15 | async-start | bytes 2621440 | tf_op jit(solution)/shard_map/all_gather | solution.py:173
  11.4 190.9 %copy-start.128 = (f32[1,1,512]{2,0,1:T(1,128)}, f32[1,1,512]{2,0,1:T(1,128)S(1)}, u32[]{:S(2)}) copy-start(f32[1,1,512]{2,0,1:T(1,128)S(1)} %get-tuple-element.226) | copy-start | bytes 6148
  14.9 85.9 %reduce-scatter.16.cloned.1.call-start = ((), (), s32[]{:S(2)}) async-start(), calls=%async_computation.16 | async-start | bytes 2621440 | tf_op jit(solution)/shard_map/reduce_scatter | solution.py:177
  65.5 75.0 %all-gather.15.cloned.1.call-start = ((), (), s32[]{:S(2)}) async-start(), calls=%async_computation.17 | async-start | bytes 2621440 | tf_op jit(solution)/shard_map/all_gather | solution.py:173
  105.0 95.5 %reduce-scatter.18.cloned.1.call-start = ((), (), s32[]{:S(2)}) async-start(), calls=%async_computation.18 | async-start | bytes 2621440 | tf_op jit(solution)/shard_map/reduce_scatter | solution.py:177
  165.1 74.4 %all-gather.17.cloned.1.call-start = ((), (), s32[]{:S(2)}) async-start(), calls=%async_computation.19 | async-start | bytes 2621440 | tf_op jit(solution)/shard_map/all_gather | solution.py:217
  204.1 79.0 %reduce-scatter.20.cloned.1.call-start = ((), (), s32[]{:S(2)}) async-start(), calls=%async_computation.20 | async-start | bytes 2621440 | tf_op jit(solution)/shard_map/reduce_scatter | solution.py:228
  247.7 75.1 %all-gather.19.cloned.1.call-start = ((), (), s32[]{:S(2)}) async-start(), calls=%async_computation.21 | async-start | bytes 2621440 | tf_op jit(solution)/shard_map/all_gather | solution.py:173
  287.3 98.5 %reduce-scatter.22.cloned.1.call-start = ((), (), s32[]{:S(2)}) async-start(), calls=%async_computation.22 | async-start | bytes 2621440 | tf_op jit(solution)/shard_map/reduce_scatter | solution.py:177
  350.5 75.1 %all-gather.21.cloned.1.call-start = ((), (), s32[]{:S(2)}) async-start(), calls=%async_computation.23 | async-start | bytes 2621440 | tf_op jit(solution)/shard_map/all_gather | solution.py:173
  390.1 110.6 %reduce-scatter.24.cloned.1.call-start = ((), (), s32[]{:S(2)}) async-start(), calls=%async_computation.24 | async-start | bytes 2621440 | tf_op jit(solution)/shard_map/reduce_scatter | solution.py:177
  465.4 74.4 %all-gather.23.cloned.1.call-start = ((), (), s32[]{:S(2)}) async-start(), calls=%async_computation.25 | async-start | bytes 2621440 | tf_op jit(solution)/shard_map/all_gather | solution.py:217
  504.4 72.7 %all-gather.25.cloned.1.call-start = ((), (), s32[]{:S(2)}) async-start(), calls=%async_computation.27 | async-start | bytes 2621440 | tf_op jit(solution)/shard_map/all_gather | solution.py:239
  507.9 115.9 %reduce-scatter.28.cloned.1.call-start = ((), (), s32[]{:S(2)}) async-start(), calls=%async_computation.28 | async-start | bytes 2621440 | tf_op jit(solution)/shard_map/reduce_scatter | solution.py:248
  588.4 78.2 %all-gather.27.cloned.1.call-start = ((), (), s32[]{:S(2)}) async-start(), calls=%async_computation.29 | async-start | bytes 2621440 | tf_op jit(solution)/shard_map/all_gather | solution.py:192
  631.2 114.0 %reduce-scatter.30.cloned.1.call-start = ((), (), s32[]{:S(2)}) async-start(), calls=%async_computation.30 | async-start | bytes 2621440 | tf_op jit(solution)/shard_map/reduce_scatter | solution.py:208
  709.8 73.7 %reduce-scatter.26.cloned.1.call-start = ((), (), s32[]{:S(2)}) async-start(), calls=%async_computation.26 | async-start | bytes 2621440 | tf_op jit(solution)/shard_map/reduce_scatter | solution.py:228
  715.8 107.5 %all-gather.29.cloned.1.call-start = ((), (), s32[]{:S(2)}) async-start(), calls=%async_computation.31 | async-start | bytes 2621440 | tf_op jit(solution)/shard_map/all_gather | solution.py:192
  787.9 99.1 %reduce-scatter.32.cloned.1.call-start = ((), (), s32[]{:S(2)}) async-start(), calls=%async_computation.32 | async-start | bytes 2621440 | tf_op jit(solution)/shard_map/reduce_scatter | solution.py:208
  851.6 77.4 %all-gather.31.cloned.1.call-start = ((), (), s32[]{:S(2)}) async-start(), calls=%async_computation.33 | async-start | bytes 2621440 | tf_op jit(solution)/shard_map/all_gather | solution.py:239
  893.6 82.3 %reduce-scatter.34.cloned.1.call-start = ((), (), s32[]{:S(2)}) async-start(), calls=%async_computation.34 | async-start | bytes 2621440 | tf_op jit(solution)/shard_map/reduce_scatter | solution.py:248
  940.6 79.3 %all-gather.33.cloned.1.call-start = ((), (), s32[]{:S(2)}) async-start(), calls=%async_computation.35 | async-start | bytes 2621440 | tf_op jit(solution)/shard_map/all_gather | solution.py:192
  984.4 103.3 %reduce-scatter.36.cloned.1.call-start = ((), (), s32[]{:S(2)}) async-start(), calls=%async_computation.36 | async-start | bytes 2621440 | tf_op jit(solution)/shard_map/reduce_scatter | solution.py:208
  1052.4 77.6 %all-gather.35.cloned.1.call-start = ((), (), s32[]{:S(2)}) async-start(), calls=%async_computation.37 | async-start | bytes 2621440 | tf_op jit(solution)/shard_map/all_gather | solution.py:192
  1094.5 72.8 %reduce-scatter.44.cloned.1.call-start = ((), (), s32[]{:S(2)}) async-start(), calls=%async_computation.41 | async-start | bytes 1179648 | tf_op jit(solution)/shard_map/reduce_scatter | solution.py:383
  1109.3 87.4 %reduce-scatter.42.cloned.1.call-start = ((), (), s32[]{:S(2)}) async-start(), calls=%async_computation.40 | async-start | bytes 884736 | tf_op jit(solution)/shard_map/reduce_scatter | solution.py:377
  1127.6 133.1 %all-reduce.7.cloned.1.call-start = ((), (), s32[]{:S(2)}) async-start(), calls=%async_computation.42 | async-start | bytes 3145728
  1151.8 142.1 %reduce-scatter.40.cloned.1.call-start = ((), (), s32[]{:S(2)}) async-start(), calls=%async_computation.39 | async-start | bytes 884736 | tf_op jit(solution)/shard_map/reduce_scatter | solution.py:371
  1160.1 170.3 %reduce-scatter.38.cloned.1.call-start = ((), (), s32[]{:S(2)}) async-start(), calls=%async_computation.38 | async-start | bytes 2621440 | tf_op jit(solution)/shard_map/reduce_scatter | solution.py:208
  1164.1 166.3 %copy-start.90 = (f32[2,32,8]{1,2,0:T(8,128)S(1)}, f32[2,32,8]{1,2,0:T(8,128)}, u32[]{:S(2)}) copy-start(f32[2,32,8]{1,2,0:T(8,128)} %copy-done.89) | copy-start | bytes 6148
  1198.4 176.5 %copy-start.26 = (f32[2,32,8,512]{3,1,2,0:T(8,128)S(1)}, f32[2,32,8,512]{3,1,2,0:T(8,128)}, u32[]{:S(2)}) copy-start(f32[2,32,8,512]{3,1,2,0:T(8,128)} %get-tuple-element.185) | copy-start | bytes 3145732
  1198.4 176.5 %copy-start.37 = (bf16[2,32,8,512]{3,1,2,0:T(8,128)(2,1)S(1)}, bf16[2,32,8,512]{3,1,2,0:T(8,128)(2,1)}, u32[]{:S(2)}) copy-start(bf16[2,32,8,512]{3,1,2,0:T(8,128)(2,1)} %reduce-scatter.36.cloned.1.call-done) | copy-start | bytes 1572868
  (165 other events, 4077.8 us)
Sparse Core Ops, SparseCore 0:
  15.0 38.0 all-gather.12
  65.6 35.1 reduce-scatter.15
  105.1 35.2 all-gather.14
  165.3 35.1 reduce-scatter.17
  204.2 35.2 all-gather.16
  247.8 35.1 reduce-scatter.19
  287.4 35.2 all-gather.18
  350.6 35.1 reduce-scatter.21
  390.2 35.2 all-gather.20
  465.5 35.1 reduce-scatter.23
  504.5 35.2 all-gather.22
  541.7 35.2 all-gather.24
  588.6 35.1 reduce-scatter.27
  631.3 35.2 all-gather.26
  709.9 35.1 reduce-scatter.29
  748.2 35.1 reduce-scatter.25
  788.0 35.2 all-gather.28
  851.8 35.1 reduce-scatter.31
  893.7 35.3 all-gather.30
  940.7 35.1 reduce-scatter.33
  984.6 35.2 all-gather.32
  1052.5 35.1 reduce-scatter.35
  1094.6 35.3 all-gather.34
  1132.2 32.3 reduce-scatter.43
  1166.9 29.6 reduce-scatter.41
  1200.2 60.4 all-reduce.6
  1262.8 31.0 reduce-scatter.39
  1297.1 33.2 reduce-scatter.37
where the time goes:
time: 1400 us; the launch traced here: 1390 us
  waiting for transfers between devices  916 us (65%)
  matrix products  163 us (12%)
  local copies, waits for them, and re-layouts  159 us (11%)
  other arithmetic  86.3 us (6%)
  blocking collectives  40.1 us (3%)
  between operations  17.6 us (1%)
    all_gather x4, waiting for transfers between devices, attention_forward(): gathered = lax.all_gather(normed, 'tensor', axis=1, tiled=True)  144 us
    reduce_scatter x4, waiting for transfers between devices, attention_forward(): lax.psum_scatter(partial_out.reshape(gathered.shape).astype(jnp.bfloat16)...  141 us
    reduce_scatter x4, waiting for transfers between devices, attention_backward(): lax.psum_scatter(normed_grad.astype(jnp.bfloat16), 'tensor', scatter_dime...  134 us
    all_gather x4, waiting for transfers between devices, attention_backward(): grad_rows = lax.all_gather(grad_low, 'tensor', axis=1, tiled=True)  107 us
    reduce_scatter x2, waiting for transfers between devices, mlp_backward(): lax.psum_scatter(normed_grad.astype(jnp.bfloat16), 'tensor', scatter_dime...  70.6 us
    reduce_scatter x2, waiting for transfers between devices, mlp_forward(): lax.psum_scatter(partial_out.astype(jnp.bfloat16), 'tensor', scatter_dime...  67.6 us
    all_gather x2, waiting for transfers between devices, mlp_backward(): grad_rows = lax.all_gather(grad_low, 'tensor', axis=1, tiled=True)  67.6 us
    all_gather x2, waiting for transfers between devices, mlp_forward(): rows_in = lax.all_gather(normed, 'tensor', axis=1, tiled=True)  64.6 us
  transfers between devices with their start and end apart: 28, of which 27 were waited for; matrix products, arithmetic and copies ran while one was open for 7% of the time, Pallas kernels for 0%

commit v1 on v0

v1 whole, which is shorter than its diff:
```python
import functools

import jax
import jax.numpy as jnp
from jax import lax
from jax.experimental import pallas as pl
from jax.experimental.pallas import tpu as pltpu
from jax.sharding import PartitionSpec as P

HD = 64
L = 2
PIECES = 4
PAIR = 2 * HD
QKV = 3 * PAIR
TILE = 128

epsilon = 1e-05
masked_score = -1e30
SCALE = HD ** (-0.5)
F32 = jnp.float32
BF = jnp.bfloat16
NT = (((1,), (1,)), ((), ()))
TN = (((0,), (0,)), ((), ()))
TANH_A = 0.7978845608028654
TANH_B = 0.044715
VMEM = pl.BlockSpec(memory_space=pltpu.VMEM)
SMEM = pl.BlockSpec(memory_space=pltpu.SMEM)
ANY = pl.BlockSpec(memory_space=pl.ANY)


class Sizes:
    def __init__(self, shape, tensor, dp):
        self.blocks, self.samples, self.feats, self.width = shape
        self.tensor, self.dp = tensor, dp
        self.rows = self.blocks * self.samples * self.feats
        self.own_feats = self.feats // tensor
        self.run = self.blocks * self.samples
        self.chunk = self.own_feats * self.run
        self.group = tensor * self.run
        self.block_rows = self.samples * self.feats
        self.fast = tensor == 4 and dp == 8


def places(z):
    tensor_at = lax.axis_index("tensor")
    dp_at = lax.axis_index("dp")
    return tensor_at, lax.rem(dp_at, 2), lax.div(dp_at, 2)


def dot(a, b):
    return jnp.dot(a, b, preferred_element_type=F32)


def dot_nt(a, b):
    return lax.dot_general(a, b, NT, preferred_element_type=F32)


def dot_tn(a, b):
    return lax.dot_general(a, b, TN, preferred_element_type=F32)


def normal_rows(x):
    centre = x - jnp.mean(x, axis=-1, keepdims=True)
    spread = jnp.mean(centre * centre, axis=-1, keepdims=True)
    rate = lax.rsqrt(spread + epsilon)
    return centre * rate, rate


def over_rows(rows, fn, carry=0, step=64):
    def one(at, kept):
        return fn(pl.ds(pl.multiple_of(at * step, step), step), kept)

    return lax.fori_loop(0, rows // step, one, carry)


def fold(x):
    return jnp.sum(x.reshape(-1, 8, x.shape[-1]), axis=0)


def total(x):
    return jnp.sum(x, axis=0, keepdims=True)


def put_strips(strips, rows, value):
    for lane in range(value.shape[1] // TILE):
        strips[lane, rows, :] = value[:, lane * TILE : (lane + 1) * TILE]


def get_strips(strips, rows):
    return jnp.concatenate([strips[lane, rows, :] for lane in range(strips.shape[0])], axis=1)


def feature_slot(sz, tensor_at, at, slot):
    return (tensor_at ^ at) * sz.own_feats + slot


def spread_out(sz, tensor_at, wide, chunks):
    for at in range(sz.tensor):
        for slot in range(sz.own_feats):
            first = feature_slot(sz, tensor_at, at, slot)
            for lane in range(sz.width // TILE):
                rows = wide[lane, pl.ds(first, sz.run, stride=sz.feats), :]
                chunks[at][
                    slot * sz.run : (slot + 1) * sz.run, lane * TILE : (lane + 1) * TILE
                ] = rows.astype(BF)


def bring_back(sz, tensor_at, chunks, wide):
    for at in range(sz.tensor):
        for slot in range(sz.own_feats):
            first = feature_slot(sz, tensor_at, at, slot)
            for lane in range(sz.width // TILE):
                rows = chunks[at][
                    slot * sz.run : (slot + 1) * sz.run, lane * TILE : (lane + 1) * TILE
                ]
                wide[lane, pl.ds(first, sz.run, stride=sz.feats), :] = rows.astype(F32)


def by_feature(sz, chunks, x):
    for at in range(sz.tensor):
        for slot in range(sz.own_feats):
            first = slot * sz.group + at * sz.run
            x[first : first + sz.run, :] = chunks[at][slot * sz.run : (slot + 1) * sz.run, :]


def to_chunks(sz, value, chunks):
    for at in range(sz.tensor):
        for slot in range(sz.own_feats):
            first = slot * sz.group + at * sz.run
            chunks[at][slot * sz.run : (slot + 1) * sz.run, :] = value[
                first : first + sz.run
            ].astype(BF)


def where_halves(core):
    other = 1 - core
    return (
        (1 + core, core),
        (2 - core, core),
        (3, core),
        (1 + other, other),
        (2 - other, other),
        (3, other),
    )


def load_unit(sz, parts, w, sems, core):
    copies = []
    if not sz.fast:
        copies.append(pltpu.make_async_copy(parts[0], w, sems.at[0]))
    else:
        copies.append(pltpu.make_async_copy(parts[0], w.at[0], sems.at[0]))
        half_rows = sz.width // 2
        for at, (piece, half) in enumerate(where_halves(core)):
            rows = pl.ds(pl.multiple_of(half * half_rows, half_rows), half_rows)
            copies.append(
                pltpu.make_async_copy(parts[at + 1], w.at[piece, rows, :], sems.at[at + 1])
            )
    for copy in copies:
        copy.start()
    return copies


def load_mlp(sz, layer_at, parts, up, down, sems, core):
    copies = []
    if not sz.fast:
        copies.append(pltpu.make_async_copy(parts[0], up, sems.at[0]))
        copies.append(pltpu.make_async_copy(parts[1], down, sems.at[1]))
    else:
        copies.append(pltpu.make_async_copy(parts[0].at[layer_at], up.at[0], sems.at[0]))
        copies.append(pltpu.make_async_copy(parts[1].at[layer_at], down.at[0], sems.at[1]))
        half_rows = sz.width // 2
        for at, (piece, half) in enumerate(where_halves(core)):
            rows = pl.ds(pl.multiple_of(half * half_rows, half_rows), half_rows)
            for member, w in enumerate((up, down)):
                copies.append(
                    pltpu.make_async_copy(
                        parts[at + 2].at[member],
                        w.at[piece, rows, :],
                        sems.at[2 + 2 * at + member],
                    )
                )
    for copy in copies:
        copy.start()
    return copies


def out_matrix(w, w_out):
    for piece in range(PIECES):
        for at in range(PIECES):
            w_out[piece * PAIR : (piece + 1) * PAIR, at * TILE : (at + 1) * TILE] = w[
                piece, at * TILE : (at + 1) * TILE, QKV:
            ]


def put_grad(sz, grads, outs, piece, member, core, z):
    if not sz.fast:
        outs[0][piece, member] = grads[...]
        return
    mine, theirs = outs
    if piece in (0, 3):
        at_mine = at_theirs = piece
    elif piece == 1:
        at_mine, at_theirs = 1 + core, 2 - core
    else:
        at_mine, at_theirs = 2 - core, 1 + core
    for near in range(4):
        first = (z ^ near) * 128
        rows_mine = pl.ds(pl.multiple_of(first + core * 64, 64), 64)
        rows_theirs = pl.ds(pl.multiple_of(first + (1 - core) * 64, 64), 64)
        mine[at_mine, near, member] = grads[rows_mine, :]
        theirs[at_theirs, near, member] = grads[rows_theirs, :]


def head_masks():
    lane = lax.broadcasted_iota(jnp.int32, (1, PAIR), 1)
    return lane < HD, lane >= HD


def sample_bias(sz, tensor_at, tasks, lengths, bias):
    def of(index):
        run_at = index // sz.run
        block = (index // sz.samples) % sz.blocks
        sample = (run_at ^ tensor_at) * sz.samples + index % sz.samples
        task = jnp.zeros_like(index)
        length = jnp.zeros_like(index)
        for at in range(sz.blocks):
            task = jnp.where(block == at, tasks[at], task)
            length = jnp.where(block == at, lengths[at], length)
        return task, sample < length

    row_task, unused = of(lax.broadcasted_iota(jnp.int32, (sz.group, 1), 0))
    key_task, key_live = of(lax.broadcasted_iota(jnp.int32, (1, sz.group), 1))
    key_task = jnp.where(key_live, key_task, -1)
    bias[...] = jnp.where(row_task == key_task, 0.0, masked_score)


def feature_bias(sz, length):
    row = lax.broadcasted_iota(jnp.int32, (TILE, TILE), 0)
    key = lax.broadcasted_iota(jnp.int32, (TILE, TILE), 1)
    same = (row // sz.feats) == (key // sz.feats)
    return jnp.where(same & (key % sz.feats < length), 0.0, masked_score)


def attend(proj, piece, rows, bias, probs, probs_at):
    first_head, second_head = head_masks()
    query = proj[piece, rows, :PAIR]
    key = proj[piece, rows, PAIR : 2 * PAIR]
    value = proj[piece, rows, 2 * PAIR :]
    mixed = []
    for head, mask in enumerate((first_head, second_head)):
        scores = dot_nt(jnp.where(mask, query, 0) * SCALE, key) + bias
        top = jnp.max(scores, axis=-1, keepdims=True)
        weights = jnp.exp(scores - top)
        weights = weights * (1.0 / jnp.sum(weights, axis=-1, keepdims=True))
        weights = weights.astype(BF)
        probs[probs_at + (head,)] = weights
        mixed.append(dot(weights, value))
    return jnp.where(first_head, mixed[0], mixed[1]).astype(BF)


def attend_back(proj, piece, rows, probs, probs_at, mixed_grad, proj_grad):
    first_head, second_head = head_masks()
    query = proj[piece, rows, :PAIR]
    key = proj[piece, rows, PAIR : 2 * PAIR]
    value = proj[piece, rows, 2 * PAIR :]
    query_grad, key_grad, value_grad = [], [], []
    for head, mask in enumerate((first_head, second_head)):
        weights = probs[probs_at + (head,)]
        head_grad = jnp.where(mask, mixed_grad, 0)
        weight_grad = dot_nt(head_grad, value)
        wide = weights.astype(F32)
        product = wide * weight_grad
        score_grad = product - wide * jnp.sum(product, axis=-1, keepdims=True)
        score_low = score_grad.astype(BF)
        value_grad.append(dot_tn(weights, head_grad))
        query_grad.append(dot(score_low, key))
        key_grad.append(dot_tn(score_low, jnp.where(mask, query, 0)))
    queries = jnp.where(first_head, query_grad[0], query_grad[1]) * SCALE
    proj_grad[piece, rows, :PAIR] = queries.astype(BF)
    proj_grad[piece, rows, PAIR : 2 * PAIR] = ((key_grad[0] + key_grad[1]) * SCALE).astype(BF)
    proj_grad[piece, rows, 2 * PAIR :] = (value_grad[0] + value_grad[1]).astype(BF)


def norm_back_rows(state, incoming, gain):
    xhat, rate = normal_rows(state)
    inner = incoming * gain
    back = rate * (
        inner
        - jnp.mean(inner, axis=-1, keepdims=True)
        - xhat * jnp.mean(inner * xhat, axis=-1, keepdims=True)
    )
    return xhat, back


def first_norm_kernel(sz, tokens, gains, shifts, *rest):
    chunks, (wide,) = rest[: sz.tensor], rest[sz.tensor :]
    tensor_at, core, z = places(sz)

    def rows_of(rows, kept):
        xhat, unused = normal_rows(tokens[rows, :].astype(F32))
        put_strips(wide, rows, xhat * gains[0, 0:1, :] + shifts[0, 0:1, :])
        return kept

    over_rows(sz.rows, rows_of)
    spread_out(sz, tensor_at, wide, chunks)


def pack_kernel(sz, units, with_mlp, *rest):
    sems = rest[-1]
    at = 2 * len(units)
    outs = rest[at + (2 if with_mlp else 0) : -1]
    tensor_at, core, z = places(sz)
    half = sz.width // 2
    started = []

    def go(source, target):
        copy = pltpu.make_async_copy(source, target, sems.at[len(started)])
        copy.start()
        started.append(copy)

    half_rows = pl.ds(pl.multiple_of(core * half, half), half)
    for unit, layer_at in enumerate(units):
        qkv, out = rest[2 * unit], rest[2 * unit + 1]
        own, sent = outs[2 * unit], outs[2 * unit + 1]
        for member in range(3):
            lanes = pl.ds(member * PAIR, PAIR)
            go(qkv.at[layer_at, member], own.at[:, lanes])
            go(qkv.at[layer_at, member, half_rows, :], sent.at[:, lanes])
        for block in range(PIECES):
            go(
                out.at[layer_at, :, pl.ds(block * TILE, TILE)],
                own.at[pl.ds(block * TILE, TILE), pl.ds(QKV, PAIR)],
            )
        for block in range(PIECES // 2):
            lanes = pl.ds(pl.multiple_of(core * half + block * TILE, TILE), TILE)
            go(
                out.at[layer_at, :, lanes],
                sent.at[pl.ds(block * TILE, TILE), pl.ds(QKV, PAIR)],
            )
    if with_mlp:
        up, down = rest[at], rest[at + 1]
        for layer_at in range(L):
            for member, w in enumerate((up, down)):
                go(w.at[layer_at, half_rows, :], outs[2 * len(units) + layer_at].at[member])
    for copy in started:
        copy.wait()


def sample_kernel(sz, tasks, lengths, *rest):
    n = sz.tensor
    parts = 7 if sz.fast else 1
    chunks, weights = rest[:n], rest[n : n + parts]
    outs = rest[n + parts :]
    back, proj, mixed, probs = outs[:n], outs[n], outs[n + 1], outs[n + 2]
    x, w, w_out, bias, sems = outs[n + 3 :]
    tensor_at, core, z = places(sz)
    copies = load_unit(sz, weights, w, sems, core)
    by_feature(sz, chunks, x)
    sample_bias(sz, tensor_at, tasks, lengths, bias)
    for copy in copies:
        copy.wait()
    out_matrix(w, w_out)
    for piece in range(PIECES):
        proj[piece] = dot(x[...], w[piece, :, :QKV]).astype(BF)
        for slot in range(sz.own_feats):
            rows = slice(slot * sz.group, (slot + 1) * sz.group)
            mixed[rows, piece * PAIR : (piece + 1) * PAIR] = attend(
                proj, piece, rows, bias[...], probs, (piece, slot)
            )
    to_chunks(sz, dot(mixed[...], w_out[...]), back)


def feature_kernel(sz, layer_at, lengths, state, gains, shifts, out_bias, *rest):
    n = sz.tensor
    parts = 7 if sz.fast else 1
    chunks, weights = rest[:n], rest[n : n + parts]
    state_1, state_2, normed_m, proj, mixed, probs = rest[n + parts : n + parts + 6]
    strips, wide, normed, w, w_out, sems = rest[n + parts + 6 :]
    tensor_at, core, z = places(sz)
    copies = load_unit(sz, weights, w, sems, core)
    bring_back(sz, tensor_at, chunks, strips)
    at = slice(layer_at, layer_at + 1)

    def before(rows, kept):
        value = state[rows, :].astype(F32) + get_strips(strips, rows) + out_bias[0, at, :]
        state_1[rows, :] = value
        xhat, unused = normal_rows(value)
        normed[rows, :] = (xhat * gains[1, at, :] + shifts[1, at, :]).astype(BF)
        return kept

    over_rows(sz.rows, before)
    biases = [feature_bias(sz, lengths[block]) for block in range(sz.blocks)]
    for copy in copies:
        copy.wait()
    out_matrix(w, w_out)
    for piece in range(PIECES):
        proj[piece] = dot(normed[...], w[piece, :, :QKV]).astype(BF)
        for tile in range(sz.rows // TILE):
            rows = slice(tile * TILE, (tile + 1) * TILE)
            mixed[rows, piece * PAIR : (piece + 1) * PAIR] = attend(
                proj, piece, rows, biases[tile * TILE // sz.block_rows], probs, (piece, tile)
            )
    wide[...] = dot(mixed[...], w_out[...])

    def after(rows, kept):
        value = state_1[rows, :] + wide[rows, :] + out_bias[1, at, :]
        state_2[rows, :] = value
        xhat, unused = normal_rows(value)
        normed_m[rows, :] = (xhat * gains[2, at, :] + shifts[2, at, :]).astype(BF)
        return kept

    over_rows(sz.rows, after)


def up_bias_rows(sz, tensor_at, piece):
    return (tensor_at ^ piece) if sz.fast else piece


def mlp_kernel(sz, layer_at, state_2, normed_m, up_bias, gains, shifts, out_bias, *rest):
    n = sz.tensor
    parts = 8 if sz.fast else 2
    weights, (state_3, *chunks) = rest[:parts], rest[parts : parts + 1 + n]
    strips, wide, up, down, sems = rest[parts + 1 + n :]
    tensor_at, core, z = places(sz)
    for copy in load_mlp(sz, layer_at, weights, up, down, sems, core):
        copy.wait()
    for piece in range(PIECES):
        shift = up_bias[layer_at, pl.ds(up_bias_rows(sz, tensor_at, piece), 1), :]
        value = dot(normed_m[...], up[piece]) + shift
        hidden = 0.5 * value * (1.0 + jnp.tanh(TANH_A * (value + TANH_B * value * value * value)))
        term = dot(hidden.astype(BF), down[piece])
        wide[...] = term if piece == 0 else wide[...] + term
    at = slice(layer_at, layer_at + 1)
    later = slice(layer_at + 1, layer_at + 2)

    def after(rows, kept):
        value = state_2[rows, :] + wide[rows, :] + out_bias[2, at, :]
        state_3[rows, :] = value
        xhat, unused = normal_rows(value)
        put_strips(strips, rows, xhat * gains[0, later, :] + shifts[0, later, :])
        return kept

    over_rows(sz.rows, after)
    spread_out(sz, tensor_at, strips, chunks)


def mlp_back(
    sz, layer_at, grad, state_2, normed_m, up_bias, gains, up, down, low, wide, wide_out, grads,
    grad_out, outs, small,
):
    tensor_at, core, z = places(sz)
    at = slice(layer_at, layer_at + 1)

    def lower(rows, kept):
        part = grad[rows, :].astype(BF)
        low[rows, :] = part
        return kept + fold(part.astype(F32))

    small[...] = jnp.zeros_like(small)
    small[2:3, :] = total(over_rows(sz.rows, lower, jnp.zeros((8, sz.width), F32)))
    for piece in range(PIECES):
        name = up_bias_rows(sz, tensor_at, piece)
        value = dot(normed_m[...], up[piece]) + up_bias[layer_at, pl.ds(name, 1), :]
        square = value * value
        bend = jnp.tanh(TANH_A * (value + TANH_B * square * value))
        hidden = (0.5 * value * (1.0 + bend)).astype(BF)
        slope = 0.5 * (1.0 + bend) + 0.5 * value * (1.0 - bend * bend) * (
            TANH_A * (1.0 + 3.0 * TANH_B * square)
        )
        if wide_out is not None:
            term = dot(hidden, down[piece])
            wide_out[...] = term if piece == 0 else wide_out[...] + term
        up_grad = (dot_nt(low[...], down[piece]) * slope).astype(BF)
        small[pl.ds(3 + name, 1), :] = total(fold(up_grad.astype(F32)))
        term = dot_nt(up_grad, up[piece])
        wide[...] = term if piece == 0 else wide[...] + term
        grads[...] = dot_tn(normed_m[...], up_grad).astype(BF)
        put_grad(sz, grads, outs, piece, 0, core, z)
        grads[...] = dot_tn(low[...], hidden).astype(BF)
        put_grad(sz, grads, outs, piece, 1, core, z)

    def back(rows, kept):
        incoming = wide[rows, :]
        xhat, change = norm_back_rows(state_2[rows, :], incoming, gains[2, at, :])
        grad_out[rows, :] = grad[rows, :] + change
        return kept[0] + fold(incoming * xhat), kept[1] + fold(incoming)

    nothing = jnp.zeros((8, sz.width), F32)
    gain_sum, shift_sum = over_rows(sz.rows, back, (nothing, nothing))
    small[0:1, :] = total(gain_sum)
    small[1:2, :] = total(shift_sum)


def last_mlp_kernel(
    sz, layer_at, sample_lens, feature_lens, cotangent, state_2, normed_m, up_bias, gains, out_bias,
    *rest,
):
    parts = 8 if sz.fast else 2
    halves = 2 if sz.fast else 1
    weights, rest = rest[:parts], rest[parts:]
    output, grad_out, small = rest[:3]
    outs = rest[3 : 3 + halves]
    grad, wide, wide_out, low, grads, up, down, sems = rest[3 + halves :]
    tensor_at, core, z = places(sz)
    copies = load_mlp(sz, layer_at, weights, up, down, sems, core)
    step = 64

    def live_rows(rows, kept):
        index = kept + lax.broadcasted_iota(jnp.int32, (step, 1), 0)
        block = index // sz.block_rows
        sample = tensor_at * sz.samples + (index // sz.feats) % sz.samples
        sample_len = jnp.zeros_like(index)
        feature_len = jnp.zeros_like(index)
        for at in range(sz.blocks):
            sample_len = jnp.where(block == at, sample_lens[at], sample_len)
            feature_len = jnp.where(block == at, feature_lens[at], feature_len)
        live = (sample < sample_len) & (index % sz.feats < feature_len)
        grad[rows, :] = jnp.where(live, cotangent[rows, :].astype(F32), 0.0)
        return kept + step

    over_rows(sz.rows, live_rows, 0, step)
    for copy in copies:
        copy.wait()
    mlp_back(
        sz, layer_at, grad, state_2, normed_m, up_bias, gains, up, down, low, wide, wide_out,
        grads, grad_out, outs, small,
    )
    at = slice(layer_at, layer_at + 1)

    def after(rows, kept):
        value = state_2[rows, :] + wide_out[rows, :] + out_bias[2, at, :]
        output[rows, :] = value.astype(BF)
        return kept

    over_rows(sz.rows, after)


def mlp_back_kernel(
    sz, layer_at, grad_in, state_3, state_2, normed_m, up_bias, gains, *rest
):
    n = sz.tensor
    parts = 8 if sz.fast else 2
    halves = 2 if sz.fast else 1
    chunks, weights, rest = rest[:n], rest[n : n + parts], rest[n + parts :]
    grad_out, small, small_s = rest[:3]
    outs = rest[3 : 3 + halves]
    grad, strips, wide, low, grads, up, down, sems = rest[3 + halves :]
    tensor_at, core, z = places(sz)
    copies = load_mlp(sz, layer_at, weights, up, down, sems, core)
    sample_norm_back(
        sz, layer_at + 1, tensor_at, grad_in, state_3, chunks, gains, strips, grad, small_s
    )
    for copy in copies:
        copy.wait()
    mlp_back(
        sz, layer_at, grad, state_2, normed_m, up_bias, gains, up, down, low, wide, None,
        grads, grad_out, outs, small,
    )


def sample_norm_back(sz, layer_at, tensor_at, grad_in, state, chunks, gains, strips, grad, small):
    bring_back(sz, tensor_at, chunks, strips)
    at = slice(layer_at, layer_at + 1)

    def back(rows, kept):
        incoming = get_strips(strips, rows)
        xhat, change = norm_back_rows(state[rows, :].astype(F32), incoming, gains[0, at, :])
        grad[rows, :] = grad_in[rows, :] + change
        return kept[0] + fold(incoming * xhat), kept[1] + fold(incoming)

    nothing = jnp.zeros((8, sz.width), F32)
    gain_sum, shift_sum = over_rows(sz.rows, back, (nothing, nothing))
    small[...] = jnp.zeros_like(small)
    small[0:1, :] = total(gain_sum)
    small[1:2, :] = total(shift_sum)


def last_norm_kernel(sz, grad_in, state, gains, *rest):
    chunks, (grad, small, strips) = rest[: sz.tensor], rest[sz.tensor :]
    tensor_at, core, z = places(sz)
    sample_norm_back(sz, 0, tensor_at, grad_in, state, chunks, gains, strips, grad, small)


def feature_back_kernel(sz, layer_at, grad, state_1, proj, probs, gains, shifts, *rest):
    n = sz.tensor
    parts = 7 if sz.fast else 1
    weights, rest = rest[:parts], rest[parts:]
    grad_out, low, proj_grad, normed, small = rest[:5]
    chunks = rest[5 : 5 + n]
    mixed_grad, strips, wide, w, w_out, sems = rest[5 + n :]
    tensor_at, core, z = places(sz)
    copies = load_unit(sz, weights, w, sems, core)
    at = slice(layer_at, layer_at + 1)
    nothing = jnp.zeros((8, sz.width), F32)

    def lower(rows, kept):
        part = grad[rows, :].astype(BF)
        low[rows, :] = part
        return kept + fold(part.astype(F32))

    small[...] = jnp.zeros_like(small)
    small[2:3, :] = total(over_rows(sz.rows, lower, nothing))
    for copy in copies:
        copy.wait()
    out_matrix(w, w_out)
    mixed_grad[...] = dot_nt(low[...], w_out[...]).astype(BF)
    for piece in range(PIECES):
        for tile in range(sz.rows // TILE):
            rows = slice(tile * TILE, (tile + 1) * TILE)
            part = mixed_grad[rows, piece * PAIR : (piece + 1) * PAIR]
            attend_back(proj, piece, rows, probs, (piece, tile), part, proj_grad)
        term = dot_nt(proj_grad[piece], w[piece, :, :QKV])
        wide[...] = term if piece == 0 else wide[...] + term

    def back(rows, kept):
        incoming = wide[rows, :]
        gain = gains[1, at, :]
        xhat, change = norm_back_rows(state_1[rows, :], incoming, gain)
        value = grad[rows, :] + change
        grad_out[rows, :] = value
        put_strips(strips, rows, value)
        normed[rows, :] = (xhat * gain + shifts[1, at, :]).astype(BF)
        rounded = value.astype(BF).astype(F32)
        return (
            kept[0] + fold(incoming * xhat),
            kept[1] + fold(incoming),
            kept[2] + fold(rounded),
        )

    sums = over_rows(sz.rows, back, (nothing, nothing, nothing))
    small[0:1, :] = total(sums[0])
    small[1:2, :] = total(sums[1])
    small[3:4, :] = total(sums[2])
    spread_out(sz, tensor_at, strips, chunks)


def sample_back_kernel(sz, proj, probs, *rest):
    n = sz.tensor
    parts = 7 if sz.fast else 1
    chunks, weights, rest = rest[:n], rest[n : n + parts], rest[n + parts :]
    back, low, proj_grad = rest[:n], rest[n], rest[n + 1]
    mixed_grad, wide, w, w_out, sems = rest[n + 2 :]
    tensor_at, core, z = places(sz)
    copies = load_unit(sz, weights, w, sems, core)
    by_feature(sz, chunks, low)
    for copy in copies:
        copy.wait()
    out_matrix(w, w_out)
    mixed_grad[...] = dot_nt(low[...], w_out[...]).astype(BF)
    for piece in range(PIECES):
        for slot in range(sz.own_feats):
            rows = slice(slot * sz.group, (slot + 1) * sz.group)
            part = mixed_grad[rows, piece * PAIR : (piece + 1) * PAIR]
            attend_back(proj, piece, rows, probs, (piece, slot), part, proj_grad)
        term = dot_nt(proj_grad[piece], w[piece, :, :QKV])
        wide[...] = term if piece == 0 else wide[...] + term
    to_chunks(sz, wide[...], back)


def matrix_grad_kernel(sz, count, proj_grad, low, mixed, *rest):
    halves = 2 if sz.fast else 1
    rows, outs, rest = rest[:count], rest[count : count + halves], rest[count + halves :]
    tensor_at, core, z = places(sz)
    if count == 1:
        (grads,) = rest
        (normed,) = rows
    else:
        grads, normed = rest
        by_feature(sz, rows, normed)
    for piece in range(PIECES):
        grads[:, :QKV] = dot_tn(normed[...], proj_grad[piece]).astype(BF)
        grads[:, QKV:] = dot_tn(low[...], mixed[:, piece * PAIR : (piece + 1) * PAIR]).astype(BF)
        put_grad(sz, grads, outs, piece, 0, core, z)


def shaped(shape, dtype):
    return jax.ShapeDtypeStruct(shape, dtype)


def launch(kernel, name, operands, specs, outs, scratch, mflops, out_spec=VMEM):
    return pl.pallas_call(
        kernel,
        out_shape=outs,
        in_specs=specs,
        out_specs=[out_spec] * len(outs),
        scratch_shapes=scratch,
        name=name,
        cost_estimate=pl.CostEstimate(
            flops=int(mflops * 1e6), bytes_accessed=8_000_000, transcendentals=0
        ),
        compiler_params=pltpu.CompilerParams(vmem_limit_bytes=52 * 2**20),
    )(*operands)


def unit_scratch(sz):
    return [
        pltpu.VMEM((PIECES, sz.width, sz.width), BF),
        pltpu.VMEM((sz.width, sz.width), BF),
    ]


def grad_shapes(sz, members):
    if sz.fast:
        return [shaped((PIECES, 4, members, 64, sz.width), BF)] * 2
    return [shaped((PIECES, members, sz.width, sz.width), BF)]


def swap_cores(sz, v):
    return lax.ppermute(v, "dp", [(at, at ^ 1) for at in range(sz.dp)])


def swap_near(sz, v, distance):
    return lax.ppermute(v, "tensor", [(at, at ^ distance) for at in range(sz.tensor)])


def swap_far(sz, v, distance):
    return lax.ppermute(v, "dp", [(at, at ^ (2 * distance)) for at in range(sz.dp)])


def swap_turn(sz, v, turn):
    pairs = []
    for dp_at in range(sz.dp):
        distance = 1 + ((dp_at + turn) % 2)
        for at in range(sz.tensor):
            base = dp_at * sz.tensor
            pairs.append((base + at, base + (at ^ distance)))
    return lax.ppermute(v, ("dp", "tensor"), pairs)


def exchange(sz, chunks):
    return [chunks[0]] + [swap_near(sz, chunks[at], at) for at in range(1, sz.tensor)]


def gather_unit(sz, half):
    first = swap_turn(sz, half, 0)
    second = swap_turn(sz, half, 1)
    third = swap_turn(sz, first, 1)
    got = [first, second, third]
    return got + [swap_cores(sz, v) for v in got]


def reduce_near(sz, mine, theirs):
    other = swap_cores(sz, theirs)

    def add(*terms):
        out = terms[0].astype(F32)
        for term in terms[1:]:
            out = out + term.astype(F32)
        return out

    second = swap_turn(sz, add(mine[2:], other[2:]).astype(BF), 1)
    first = swap_turn(sz, add(mine[1], other[1], second[1]).astype(BF), 0)
    return add(mine[0], other[0], second[0], first)


def reduce_far(sz, sums):
    got = swap_far(sz, sums[2:].astype(BF), 2)
    sums = sums[:2] + got.astype(F32)
    got = swap_far(sz, sums[1].astype(BF), 1)
    return sums[0] + got.astype(F32)


def reduce_whole(sz, full):
    members, width = full.shape[1], full.shape[2]
    full = full.transpose(1, 2, 0, 3)
    part = lax.psum_scatter(full, "dp", scatter_dimension=1, tiled=True)
    return lax.psum(part, "tensor").astype(F32)


def small_sum(sz, small):
    if not sz.fast:
        return lax.psum(small, ("dp", "tensor"))
    small = small + swap_cores(sz, small)
    small = small + swap_near(sz, small, 1)
    small = small + swap_near(sz, small, 2)
    small = small + swap_far(sz, small, 1)
    return small + swap_far(sz, small, 2)


def gathered_unit(qkv, out):
    qkv = lax.all_gather(qkv, "tensor", axis=2, tiled=True)
    out = lax.all_gather(out, "tensor", axis=0, tiled=True)
    width = qkv.shape[1]
    left = qkv.reshape(3, width, PIECES, PAIR).transpose(2, 1, 0, 3).reshape(PIECES, width, QKV)
    right = out.reshape(PIECES, PAIR, PIECES, TILE).transpose(0, 2, 1, 3)
    return jnp.concatenate([left, right.reshape(PIECES, width, PAIR)], axis=2)


def body(
    tokens,
    cotangent,
    block_task,
    sample_len,
    feature_len,
    norm_gain,
    norm_shift,
    sample_qkv,
    sample_out,
    feature_qkv,
    feature_out,
    out_bias,
    up_weight,
    up_bias,
    down_weight,
):
    shape = tokens.shape
    sz = Sizes(shape, lax.axis_size("tensor"), lax.axis_size("dp"))
    rows, width, n = sz.rows, sz.width, sz.tensor
    tokens = tokens.reshape(rows, width)
    cotangent = cotangent.reshape(rows, width)
    gains, shifts, biases = (
        jnp.transpose(v, (1, 0, 2)) for v in (norm_gain, norm_shift, out_bias)
    )
    up_rows = up_bias.reshape(L, PIECES, -1)
    qkvs = [jnp.transpose(v, (0, 2, 1, 3)) for v in (sample_qkv, feature_qkv)]
    outs = [sample_out, feature_out]
    part = functools.partial
    wide = pltpu.VMEM((rows, width), F32)
    strips = pltpu.VMEM((width // TILE, rows, TILE), F32)
    slim = pltpu.VMEM((rows, width), BF)
    dma = pltpu.SemaphoreType.DMA
    row_f32 = shaped((rows, width), F32)
    row_bf = shaped((rows, width), BF)
    chunk_shapes = [shaped((sz.chunk, width), BF)] * n
    proj_shape = shaped((PIECES, rows, QKV), BF)
    small_shape = shaped((8, width), F32)

    chunks = launch(
        part(first_norm_kernel, sz), "first_norm", (tokens, gains, shifts), [VMEM] * 3,
        chunk_shapes, [strips], 1,
    )

    units = [[None, None] for _ in range(L)]
    mlps = [None] * L
    if sz.fast:
        pair = [shaped((width, width), BF), shaped((width // 2, width), BF)]
        half_mlp = shaped((2, width // 2, width), BF)
        own, sent = launch(
            part(pack_kernel, sz, (0,), False), "pack_first", (qkvs[0], outs[0]), [ANY] * 2,
            pair, [dma((12,))], 1, ANY,
        )
        units[0][0] = [own] + gather_unit(sz, sent)
        rest = [(0, 1)] + [(layer_at, kind) for layer_at in range(1, L) for kind in range(2)]
        operands = []
        for layer_at, kind in rest:
            operands += [qkvs[kind], outs[kind]]
        packed = launch(
            part(pack_kernel, sz, tuple(layer_at for layer_at, _ in rest), True), "pack_rest",
            (*operands, up_weight, down_weight), [ANY] * (len(operands) + 2),
            pair * len(rest) + [half_mlp] * L, [dma((12 * len(rest) + 2 * L,))], 1, ANY,
        )
        by_unit = {key: packed[2 * at : 2 * at + 2] for at, key in enumerate(rest)}
        for layer_at in range(L):
            for kind in range(2):
                if units[layer_at][kind] is None:
                    own, sent = by_unit[layer_at, kind]
                    units[layer_at][kind] = [own] + gather_unit(sz, sent)
            halves = gather_unit(sz, packed[2 * len(rest) + layer_at])
            mlps[layer_at] = [up_weight, down_weight] + halves
    else:
        for layer_at in range(L):
            for kind in range(2):
                units[layer_at][kind] = [
                    gathered_unit(qkvs[kind][layer_at], outs[kind][layer_at])
                ]
            up = lax.all_gather(up_weight[layer_at], "tensor", axis=1, tiled=True)
            down = lax.all_gather(down_weight[layer_at], "tensor", axis=0, tiled=True)
            up = up.reshape(width, PIECES, width).transpose(1, 0, 2)
            mlps[layer_at] = [up, down.reshape(PIECES, width, width)]
    unit_specs = [ANY] * len(units[0][0])
    mlp_specs = [ANY] * len(mlps[0])
    unit_sems, mlp_sems = dma((len(unit_specs),)), dma((2 * len(mlp_specs) - 2,))
    mlp_scratch = [pltpu.VMEM((PIECES, width, width), BF)] * 2

    state = tokens
    kept = []
    for layer_at in range(L):
        entry = state
        got = exchange(sz, chunks)
        slots = sz.own_feats
        *back, proj_s, mixed_s, probs_s = launch(
            part(sample_kernel, sz), f"sample_{layer_at}",
            (block_task, sample_len, *got, *units[layer_at][0]),
            [SMEM] * 2 + [VMEM] * n + unit_specs,
            chunk_shapes
            + [proj_shape, row_bf, shaped((PIECES, slots, 2, sz.group, sz.group), BF)],
            [slim, *unit_scratch(sz), pltpu.VMEM((sz.group, sz.group), F32), unit_sems],
            3000,
        )
        back = exchange(sz, back)
        tiles = rows // TILE
        state_1, state_2, normed_m, proj_f, mixed_f, probs_f = launch(
            part(feature_kernel, sz, layer_at), f"feature_{layer_at}",
            (feature_len, state, gains, shifts, biases, *back, *units[layer_at][1]),
            [SMEM] + [VMEM] * (4 + n) + unit_specs,
            [row_f32, row_f32, row_bf, proj_shape, row_bf,
             shaped((PIECES, tiles, 2, TILE, TILE), BF)],
            [strips, wide, slim, *unit_scratch(sz), unit_sems],
            3000,
        )
        if layer_at < L - 1:
            state, *chunks = launch(
                part(mlp_kernel, sz, layer_at), f"mlp_{layer_at}",
                (state_2, normed_m, up_rows, gains, shifts, biases, *mlps[layer_at]),
                [VMEM] * 6 + mlp_specs,
                [row_f32] + chunk_shapes,
                [strips, wide, *mlp_scratch, mlp_sems],
                3000,
            )
        kept.append((entry, got, proj_s, mixed_s, probs_s, state_1, state_2, normed_m,
                     proj_f, mixed_f, probs_f))

    pending = []
    smalls = [None] * L
    matrix_grads = {}
    for layer_at in reversed(range(L)):
        (entry, got, proj_s, mixed_s, probs_s, state_1, state_2, normed_m,
         proj_f, mixed_f, probs_f) = kept[layer_at]
        if layer_at == L - 1:
            output, grad, small_m, *parts = launch(
                part(last_mlp_kernel, sz, layer_at), f"last_mlp_{layer_at}",
                (sample_len, feature_len, cotangent, state_2, normed_m, up_rows, gains, biases,
                 *mlps[layer_at]),
                [SMEM] * 2 + [VMEM] * 6 + mlp_specs,
                [row_bf, row_f32, small_shape] + grad_shapes(sz, 2),
                [wide, wide, wide, slim, pltpu.VMEM((width, width), BF), *mlp_scratch, mlp_sems],
                7000,
            )
        else:
            grad, small_m, small_s, *parts = launch(
                part(mlp_back_kernel, sz, layer_at), f"mlp_back_{layer_at}",
                (grad, kept[layer_at + 1][0], state_2, normed_m, up_rows, gains, *back,
                 *mlps[layer_at]),
                [VMEM] * (6 + n) + mlp_specs,
                [row_f32, small_shape, small_shape] + grad_shapes(sz, 2),
                [wide, strips, wide, slim, pltpu.VMEM((width, width), BF), *mlp_scratch,
                 mlp_sems],
                7000,
            )
            smalls[layer_at + 1].append(small_s)
        matrix_grads[layer_at, 2] = parts
        grad, low, proj_grad, normed, small_f, *chunks = launch(
            part(feature_back_kernel, sz, layer_at), f"feature_back_{layer_at}",
            (grad, state_1, proj_f, probs_f, gains, shifts, *units[layer_at][1]),
            [VMEM] * 6 + unit_specs,
            [row_f32, row_bf, proj_shape, row_bf, small_shape] + chunk_shapes,
            [slim, strips, wide, *unit_scratch(sz), unit_sems],
            4000,
        )
        smalls[layer_at] = [small_m, small_f]
        chunks = exchange(sz, chunks)
        matrix_grads[layer_at, 1] = launch(
            part(matrix_grad_kernel, sz, 1), f"feature_matrix_{layer_at}",
            (proj_grad, low, mixed_f, normed), [VMEM] * 4, grad_shapes(sz, 1),
            [pltpu.VMEM((width, width), BF)], 2000,
        )
        *back, low, proj_grad = launch(
            part(sample_back_kernel, sz), f"sample_back_{layer_at}",
            (proj_s, probs_s, *chunks, *units[layer_at][0]),
            [VMEM] * (2 + n) + unit_specs,
            chunk_shapes + [row_bf, proj_shape],
            [slim, wide, *unit_scratch(sz), unit_sems],
            4000,
        )
        back = exchange(sz, back)
        matrix_grads[layer_at, 0] = launch(
            part(matrix_grad_kernel, sz, n), f"sample_matrix_{layer_at}",
            (proj_grad, low, mixed_s, *got), [VMEM] * (3 + n), grad_shapes(sz, 1),
            [pltpu.VMEM((width, width), BF), slim], 2000,
        )
    tokens_grad, small_s = launch(
        part(last_norm_kernel, sz), "last_norm", (grad, tokens, gains, *back), [VMEM] * (3 + n),
        [row_f32, small_shape], [strips], 1,
    )

    early = []
    for layer_at in range(L):
        early += smalls[layer_at]
    early = small_sum(sz, jnp.concatenate(early, axis=0)).reshape(-1, 8, width)
    late = small_sum(sz, small_s)
    by_layer = []
    at = 0
    for layer_at in range(L):
        count = len(smalls[layer_at])
        sums = [early[at + member] for member in range(count)]
        at += count
        by_layer.append(sums if count == 3 else sums + [late])
    gain_total, shift_total = (
        jnp.stack([jnp.stack([s[row], f[row], m[row]]) for m, f, s in by_layer])
        for row in range(2)
    )
    bias_total = jnp.stack([jnp.stack([f[3], f[2], m[2]]) for m, f, s in by_layer])
    up_bias_total = jnp.stack([m[3 : 3 + PIECES].reshape(-1) for m, f, s in by_layer])

    done = {}
    if sz.fast:
        for layer_at in reversed(range(L)):
            groups = [[2], [1], [0]]
            for group in groups:
                for kind in group:
                    done[layer_at, kind] = reduce_far(
                        sz, reduce_near(sz, *matrix_grads[layer_at, kind])
                    )
    else:
        for key, (full,) in matrix_grads.items():
            done[key] = reduce_whole(sz, full)

    def attention_grads(kind):
        qkv, out = [], []
        for layer_at in range(L):
            if sz.fast:
                value = done[layer_at, kind][0]
                qkv.append(value[:, :QKV].reshape(-1, 3, PAIR))
                out.append(value[:, QKV:].T)
            else:
                value = done[layer_at, kind][0]
                columns = width // n
                start = lax.axis_index("tensor") * columns
                whole = value[:, :, :QKV].reshape(-1, PIECES, 3, PAIR).transpose(0, 2, 1, 3)
                whole = whole.reshape(-1, 3, width)
                qkv.append(lax.dynamic_slice_in_dim(whole, start, columns, 2))
                whole = value[:, :, QKV:].reshape(-1, width)
                out.append(lax.dynamic_slice_in_dim(whole, start, columns, 1).T)
        return jnp.stack(qkv), jnp.stack(out)

    sample_qkv_grad, sample_out_grad = attention_grads(0)
    feature_qkv_grad, feature_out_grad = attention_grads(1)
    ups, downs = [], []
    for layer_at in range(L):
        value = done[layer_at, 2]
        if not sz.fast:
            columns = PIECES * width // n
            start = lax.axis_index("tensor") * columns
            value = value.reshape(2, -1, PIECES * width)
            value = lax.dynamic_slice_in_dim(value, start, columns, 2)
        ups.append(value[0])
        downs.append(value[1].T)
    return (
        output.reshape(shape),
        tokens_grad.reshape(shape),
        gain_total,
        shift_total,
        sample_qkv_grad,
        sample_out_grad,
        feature_qkv_grad,
        feature_out_grad,
        bias_total,
        jnp.stack(ups),
        up_bias_total,
        jnp.stack(downs),
    )


def solution(mesh):
    placed = (
        P("dp", "tensor", None, None),
        P("dp", "tensor", None, None),
        P("dp"),
        P("dp"),
        P("dp"),
        P(),
        P(),
        P(None, None, None, "tensor"),
        P(None, "tensor", None),
        P(None, None, None, "tensor"),
        P(None, "tensor", None),
        P(),
        P(None, None, "tensor"),
        P(),
        P(None, "tensor", None),
    )
    return jax.shard_map(
        body,
        mesh=mesh,
        in_specs=placed,
        out_specs=(
            P("dp", "tensor", None, None),
            P("dp", "tensor", None, None),
            P(),
            P(),
            P(None, "dp", None, "tensor"),
            P(None, "tensor", "dp"),
            P(None, "dp", None, "tensor"),
            P(None, "tensor", "dp"),
            P(),
            P(None, "dp", "tensor"),
            P(),
            P(None, "tensor", "dp"),
        ),
        check_vma=False,
    )
```

time: 1400 us -> 516 us (0.37)
  waiting for transfers between devices: 916 us -> 136 us
  Pallas kernels: 0 us -> 230 us
  matrix products: 163 us -> 0 us
  local copies, waits for them, and re-layouts: 159 us -> 27.1 us
  starting transfers between devices: 4 us -> 90 us
  other arithmetic: 86.3 us -> 21.4 us
  blocking collectives: 40.1 us -> 0 us
  between operations: 17.6 us -> 2.05 us
    reduce_scatter x15 -> x0, waiting for transfers between devices: 470 us -> none  [the longest x4 141 us: attention_forward(): lax.psum_scatter(partial_out.reshape(gathered.shape).astype(jnp.bfloat16)...]
    all_gather x12 -> x0, waiting for transfers between devices: 383 us -> none  [the longest x4 144 us: attention_forward(): gathered = lax.all_gather(normed, 'tensor', axis=1, tiled=True)]
    pallas_call x0 -> x19, Pallas kernels: none -> 230 us  [launch(): pl.pallas_call(kernel, out_shape=outs, in_specs=specs, out_specs=[out_spe...]
    dot_general x60 -> x0, matrix products: 163 us -> none  [the longest x4 15.6 us: attention_backward(): jnp.einsum('cbsfx,dcx->bsfd', proj_grad, weight, preferred_element_type=j...]
    ppermute x0 -> x100, waiting for transfers between devices: none -> 136 us  [the longest x30 52.2 us: swap_turn(): return lax.ppermute(v, ('dp', 'tensor'), pairs)]
    ppermute x0 -> x100, starting transfers between devices: none -> 90 us  [the longest x30 32.7 us: swap_turn(): return lax.ppermute(v, ('dp', 'tensor'), pairs)]
    unnamed x29 -> x0, waiting for transfers between devices: 62.8 us -> none
    reduce_sum x34 -> x0, other arithmetic: 60.5 us -> none  [the longest x12 27.3 us: layer_norm(): return centre * lax.rsqrt(spread + epsilon) * gain_row + shift_row]
  transfers between devices with their start and end apart: 28 -> 100, of which waited for: 27 -> 43; matrix products, arithmetic and copies ran while one was open for 7% -> 5% of each run, Pallas kernels for 0% -> 27%
where the time goes in v1:
time: 516 us; the launch traced here: 507 us
  Pallas kernels  230 us (45%)
  waiting for transfers between devices  136 us (26%)
  starting transfers between devices  90 us (17%)
  local copies, waits for them, and re-layouts  27.1 us (5%)
  other arithmetic  21.4 us (4%)
    pallas_call x19, Pallas kernels, launch(): pl.pallas_call(kernel, out_shape=outs, in_specs=specs, out_specs=[out_spe...  230 us
    ppermute x30, waiting for transfers between devices, swap_turn(): return lax.ppermute(v, ('dp', 'tensor'), pairs)  52.2 us
    ppermute x16, waiting for transfers between devices, swap_far(): lax.ppermute(v, 'dp', [(at, at ^ 2 * distance) for at in range(sz.dp)])  42.4 us
    ppermute x28, waiting for transfers between devices, swap_near(): lax.ppermute(v, 'tensor', [(at, at ^ distance) for at in range(sz.tensor)])  40.9 us
    ppermute x30, starting transfers between devices, swap_turn(): return lax.ppermute(v, ('dp', 'tensor'), pairs)  32.7 us
    ppermute x28, starting transfers between devices, swap_near(): lax.ppermute(v, 'tensor', [(at, at ^ distance) for at in range(sz.tensor)])  31.6 us
    unnamed x166, local copies, waits for them, and re-layouts  23.1 us
    ppermute x16, starting transfers between devices, swap_far(): lax.ppermute(v, 'dp', [(at, at ^ 2 * distance) for at in range(sz.dp)])  20.3 us
  transfers between devices with their start and end apart: 100, of which 43 were waited for; matrix products, arithmetic and copies ran while one was open for 5% of the time, Pallas kernels for 27%

profile of v1, /device:TPU:0, one launch (start us, length us, event | category | flops | bytes accessed | tf_op | source)
XLA Modules:
  0.0 506.6 jit_solution(17256261864587209547)
XLA Ops:
  17.9 57.1 %pack_rest.1 = (bf16[512,512]{1,0:T(8,128)(2,1)S(1)}, bf16[256,512]{1,0:T(8,128)(2,1)S(1)}, bf16[512,512]{1,0:T(8,128)(2,1)}, bf16[256,512]{1,0:T(8,128)(2,1)S(1...) custom-call(bf16[2,3,512,128]{3,2,1,0:T(8,128)(2,1)} %bitcast.182, ...), custom_call_target="tpu_custom_call" | custom-call | flops 1000000 | bytes 8000000 | tf_op jit(solution)/shard_map/pack_rest/pallas_call | solution.py:682
  80.4 4.7 collective-permute-done.13.rest_6_.rest_2_
  87.1 3.6 collective-permute-done.28.rest_6_
  91.4 4.9 collective-permute-done.37.rest_6_.rest_2_
  96.3 5.8 %collective-permute-done.36.rest_5_.rest_1_ = bf16[256,512]{1,0:T(8,128)(2,1)S(1)} collective-permute-done((bf16[256,512]{1,0:T(8,128)(2,1)S(1)}, bf16[256,512]{1,0:T(8,128)(2,1)S(1)}, u32[]{:S(2)}, u32[]{:S(2)}) %collective-permute-start.36) | collective-permute-done | bytes 262176 | tf_op jit(solution)/shard_map/ppermute | solution.py:728
  109.4 6.9 %sample_0.1 = (bf16[128,512]{1,0:T(8,128)(2,1)S(1)}, bf16[128,512]{1,0:T(8,128)(2,1)S(1)}, bf16[128,512]{1,0:T(8,128)(2,1)S(1)}, bf16[128,512]{1,0:T(8,128)(2,1)...) custom-call(s32[2]{0:T(128)S(1)} %copy-done.33, s32[2]{0:T(128)S(1)} %copy-done.34, ...), custom_call_target="tpu_custom_call" | custom-call | flops 3000000000 | bytes 8000000 | tf_op jit(solution)/shard_map/sample_0/pallas_call | solution.py:682
  128.8 6.2 %collective-permute-done.11.rest_3_ = bf16[128,512]{1,0:T(8,128)(2,1)} collective-permute-done((bf16[128,512]{1,0:T(8,128)(2,1)}, bf16[128,512]{1,0:T(8,128)(2,1)}, u32[]{:S(2)}, u32[]{:S(2)}) %collective-permute-start.11) | collective-permute-done | bytes 131104 | tf_op jit(solution)/shard_map/ppermute | solution.py:714
  139.3 18.0 %feature_0.1 = (f32[512,512]{1,0:T(8,128)}, f32[512,512]{1,0:T(8,128)}, bf16[512,512]{1,0:T(8,128)(2,1)}, bf16[4,512,384]{2,1,0:T(8,128)(2,1)}, bf16[512,512]{1,...) custom-call(s32[2]{0:T(128)S(1)} %copy-done.35, bf16[512,512]{1,0:T(8,128)(2,1)} %bitcast.159, f32[3,2,512]{2,1,0:T(2,128)S(1)} %bitcast.163, ...), custom_call_target="tpu_custom_call" | custom-call | flops 3000000000 | bytes 8000000 | tf_op jit(solution)/shard_map/feature_0/pallas_call | solution.py:682
  162.1 8.8 %mlp_0.1 = (f32[512,512]{1,0:T(8,128)}, bf16[128,512]{1,0:T(8,128)(2,1)S(1)}, bf16[128,512]{1,0:T(8,128)(2,1)S(1)}, bf16[128,512]{1,0:T(8,128)(2,1)S(1)}, bf16[128,512]{1,0:T(8,128)(2,1)S(1)}) custom-call(f32[512,512]{1,0:T(8,128)} %get-tuple-element.119.state_2, bf16[512,512]{1,0:T(8,128)(2,1)S(1)} %copy-done.36, f32[2,4,512]{2,1,0:T(4,128)S(1)} %reshape.545.up_bias, ...), custom_call_target="tpu_custom_call" | custom-call | flops 3000000000 | bytes 8000000 | tf_op jit(solution)/shard_map/mlp_0/pallas_call | solution.py:682
  181.4 6.9 %sample_1.1 = (bf16[128,512]{1,0:T(8,128)(2,1)S(1)}, bf16[128,512]{1,0:T(8,128)(2,1)S(1)}, bf16[128,512]{1,0:T(8,128)(2,1)S(1)}, bf16[128,512]{1,0:T(8,128)(2,1)...) custom-call(s32[2]{0:T(128)S(1)} %copy-done.33, ...), custom_call_target="tpu_custom_call" | custom-call | flops 3000000000 | bytes 8000000 | tf_op jit(solution)/shard_map/sample_1/pallas_call | solution.py:682
  199.7 18.2 %feature_1.1 = (f32[512,512]{1,0:T(8,128)}, f32[512,512]{1,0:T(8,128)}, bf16[512,512]{1,0:T(8,128)(2,1)}, bf16[4,512,384]{2,1,0:T(8,128)(2,1)}, bf16[512,512]{1,...) custom-call(s32[2]{0:T(128)S(1)} %copy-done.35, f32[512,512]{1,0:T(8,128)} %get-tuple-element.122.state.state_3, ...), custom_call_target="tpu_custom_call" | custom-call | flops 3000000000 | bytes 8000000 | tf_op jit(solution)/shard_map/feature_1/pallas_call | solution.py:682
  220.2 17.0 %last_mlp_1.1 = (bf16[512,512]{1,0:T(8,128)(2,1)}, f32[512,512]{1,0:T(8,128)}, f32[8,512]{1,0:T(8,128)S(1)}, bf16[4,4,2,64,512]{4,3,2,1,0:T(8,128)(2,1)}, bf16[4,4,2,64,512]{4,3,2,1,0:T(8,128)(2,1)}) custom-call(s32[2]{0:T(128)S(1)} %copy-done.34, s32[2]{0:T(128)S(1)} %copy-done.35, bf16[512,512]{1,0:T(8,128)(2,1)S(1)} %bitcast.177, ...), custom_call_target="tpu_custom_call" | custom-call | flops 7000000000 | bytes 8000000 | tf_op jit(solution)/shard_map/last_mlp_1/pallas_call | solution.py:682
  237.2 17.3 %feature_back_1.1 = (f32[512,512]{1,0:T(8,128)}, bf16[512,512]{1,0:T(8,128)(2,1)}, bf16[4,512,384]{2,1,0:T(8,128)(2,1)}, bf16[512,512]{1,0:T(8,128)(2,1)}, f32[8...) custom-call(f32[512,512]{1,0:T(8,128)} %get-tuple-element.139.grad, ...), custom_call_target="tpu_custom_call" | custom-call | flops 4000000000 | bytes 8000000 | tf_op jit(solution)/shard_map/feature_back_1/pallas_call | solution.py:682
  262.4 9.7 %sample_back_1.1 = (bf16[128,512]{1,0:T(8,128)(2,1)S(1)}, bf16[128,512]{1,0:T(8,128)(2,1)S(1)}, bf16[128,512]{1,0:T(8,128)(2,1)S(1)}, bf16[128,512]{1,0:T(8,128)...) custom-call(bf16[4,512,384]{2,1,0:T(8,128)(2,1)} %get-tuple-element.144.proj, ...), custom_call_target="tpu_custom_call" | custom-call | flops 4000000000 | bytes 8000000 | tf_op jit(solution)/shard_map/sample_back_1/pallas_call | solution.py:682
  280.1 16.8 %mlp_back_0.1 = (f32[512,512]{1,0:T(8,128)}, f32[8,512]{1,0:T(8,128)S(1)}, f32[8,512]{1,0:T(8,128)S(1)}, bf16[4,4,2,64,512]{4,3,2,1,0:T(8,128)(2,1)}, bf16[4,4,2,64,512]{4,3,2,1,0:T(8,128)(2,1)}) custom-call(f32[512,512]{1,0:T(8,128)} %get-tuple-element.143.grad_in, f32[512,512]{1,0:T(8,128)} %get-tuple-element.122.state.state_3, ...), custom_call_target="tpu_custom_call" | custom-call | flops 7000000000 | bytes 8000000 | tf_op jit(solution)/shard_map/mlp_back_0/pallas_call | solution.py:682
  296.9 17.4 %feature_back_0.1 = (f32[512,512]{1,0:T(8,128)}, bf16[512,512]{1,0:T(8,128)(2,1)}, bf16[4,512,384]{2,1,0:T(8,128)(2,1)}, bf16[512,512]{1,0:T(8,128)(2,1)}, f32[8...) custom-call(f32[512,512]{1,0:T(8,128)} %get-tuple-element.154.grad, ...), custom_call_target="tpu_custom_call" | custom-call | flops 4000000000 | bytes 8000000 | tf_op jit(solution)/shard_map/feature_back_0/pallas_call | solution.py:682
  322.2 9.7 %sample_back_0.1 = (bf16[128,512]{1,0:T(8,128)(2,1)S(1)}, bf16[128,512]{1,0:T(8,128)(2,1)S(1)}, bf16[128,512]{1,0:T(8,128)(2,1)S(1)}, bf16[128,512]{1,0:T(8,128)...) custom-call(bf16[4,512,384]{2,1,0:T(8,128)(2,1)} %get-tuple-element.159.proj, ...), custom_call_target="tpu_custom_call" | custom-call | flops 4000000000 | bytes 8000000 | tf_op jit(solution)/shard_map/sample_back_0/pallas_call | solution.py:682
  339.9 4.8 last_norm.1
  347.3 4.7 feature_matrix_1.1
  354.8 4.8 sample_matrix_1.1
  362.0 4.8 feature_matrix_0.1
  370.1 4.8 sample_matrix_0.1
  375.5 7.1 %collective-permute-done.69 = f32[40,512]{1,0:T(8,128)S(1)} collective-permute-done((f32[40,512]{1,0:T(8,128)S(1)}, f32[40,512]{1,0:T(8,128)S(1)}, u32[]{:S(2)}, u32[]{:S(2)}) %collective-permute-start.69) | collective-permute-done | bytes 81952 | tf_op jit(solution)/shard_map/ppermute | solution.py:718
  390.0 5.2 %collective-permute-done.86 = bf16[2,4,1,64,512]{4,3,1,2,0:T(8,128)(2,1)S(1)} collective-permute-done((bf16[2,4,1,64,512]{4,3,1,2,0:T(8,128)(2,1)S(1)}, bf16[2,4,1,64,512]{4,3,1,2,0:T(8,128)(2,1)S(1)}, u32[]{:S(2)}, u32[]{:S(2)}) %collective-permute-start.86) | collective-permute-done | bytes 524320 | tf_op jit(solution)/shard_map/ppermute | solution.py:728
  396.7 4.1 collective-permute-done.76
  402.3 7.0 %collective-permute-done.81 = bf16[2,4,1,64,512]{4,3,1,2,0:T(8,128)(2,1)S(1)} collective-permute-done((bf16[2,4,1,64,512]{4,3,1,2,0:T(8,128)(2,1)S(1)}, bf16[2,4,1,64,512]{4,3,1,2,0:T(8,128)(2,1)S(1)}, u32[]{:S(2)}, u32[]{:S(2)}) %collective-permute-start.81) | collective-permute-done | bytes 524320 | tf_op jit(solution)/shard_map/ppermute | solution.py:728
  412.3 4.5 collective-permute-done.77
  417.5 6.0 %collective-permute-done.88 = bf16[2,1,64,512]{3,2,0,1:T(8,128)(2,1)S(1)} collective-permute-done((bf16[2,1,64,512]{3,2,0,1:T(8,128)(2,1)S(1)}, bf16[2,1,64,512]{3,2,0,1:T(8,128)(2,1)S(1)}, u32[]{:S(2)}, u32[]{:S(2)}) %collective-permute-start.88) | collective-permute-done | bytes 131104 | tf_op jit(solution)/shard_map/ppermute | solution.py:718
  460.4 8.6 %collective-permute-done.97 = bf16[4,2,64,512]{3,2,1,0:T(8,128)(2,1)} collective-permute-done((bf16[4,2,64,512]{3,2,1,0:T(8,128)(2,1)}, bf16[4,2,64,512]{3,2,1,0:T(8,128)(2,1)}, u32[]{:S(2)}, u32[]{:S(2)}) %collective-permute-start.97) | collective-permute-done | bytes 524320 | tf_op jit(solution)/shard_map/ppermute | solution.py:728
  474.8 7.4 %collective-permute-done.98 = bf16[2,2,64,512]{3,2,1,0:T(8,128)(2,1)S(1)} collective-permute-done((bf16[2,2,64,512]{3,2,1,0:T(8,128)(2,1)S(1)}, bf16[2,2,64,512]{3,2,1,0:T(8,128)(2,1)S(1)}, u32[]{:S(2)}, u32[]{:S(2)}) %collective-permute-start.98) | collective-permute-done | bytes 262176 | tf_op jit(solution)/shard_map/ppermute | solution.py:718
  489.3 10.4 %collective-permute-done.93 = bf16[2,2,64,512]{3,2,1,0:T(8,128)(2,1)S(1)} collective-permute-done((bf16[2,2,64,512]{3,2,1,0:T(8,128)(2,1)S(1)}, bf16[2,2,64,512]{3,2,1,0:T(8,128)(2,1)S(1)}, u32[]{:S(2)}, u32[]{:S(2)}) %collective-permute-start.93) | collective-permute-done | bytes 262176 | tf_op jit(solution)/shard_map/ppermute | solution.py:718
  499.9 4.9 collective-permute-done.94
  (436 shorter events, 186.4 us)
Async XLA Ops:
  3.8 74.6 %collective-permute-start.4 = (bf16[256,512]{1,0:T(8,128)(2,1)S(1)}, bf16[256,512]{1,0:T(8,128)(2,1)S(1)}, u32[]{:S(2)}, u32[]{:S(2)}) collective-permute-start(bf16[256,512]{1,0:T(8,128)(2,1)S(1)} %get-tuple-element.112), channel_id=1, source_target_pairs={{0,2},{1,3},{2,0},{3,1},{4,5},{5,4},{6,7},{7,6},{8,10},{9,11},{10,... | collective-permute-start | bytes 786440 | tf_op jit(solution)/shard_map/ppermute | solution.py:728
  11.0 64.9 %collective-permute-start = (bf16[128,512]{1,0:T(8,128)(2,1)S(1)}, bf16[128,512]{1,0:T(8,128)(2,1)S(1)}, u32[]{:S(2)}, u32[]{:S(2)}) collective-permute-start(bf16[128,512]{1,0:T(8,128)(2,1)S(1)} %get-tuple-element.108), channel_id=1, source_target_pairs={{0,1},{1,0},{2,3},{3,2},{4,5},{5,4},{6,7},{7,6},{8,9},{9,8},{10,11... | collective-permute-start | bytes 393224 | tf_op jit(solution)/shard_map/ppermute | solution.py:714
  12.5 63.8 %collective-permute-start.1 = (bf16[128,512]{1,0:T(8,128)(2,1)S(1)}, bf16[128,512]{1,0:T(8,128)(2,1)S(1)}, u32[]{:S(2)}, u32[]{:S(2)}) collective-permute-start(bf16[128,512]{1,0:T(8,128)(2,1)S(1)} %get-tuple-element.109), channel_id=1, source_target_pairs={{0,2},{1,3},{2,0},{3,1},{4,6},{5,7},{6,4},{7,5},{8,10},{9,11},{10,... | collective-permute-start | bytes 393224 | tf_op jit(solution)/shard_map/ppermute | solution.py:714
  13.0 63.4 %collective-permute-start.2 = (bf16[128,512]{1,0:T(8,128)(2,1)S(1)}, bf16[128,512]{1,0:T(8,128)(2,1)S(1)}, u32[]{:S(2)}, u32[]{:S(2)}) collective-permute-start(bf16[128,512]{1,0:T(8,128)(2,1)S(1)} %get-tuple-element.110), channel_id=1, source_target_pairs={{0,3},{1,2},{2,1},{3,0},{4,7},{5,6},{6,5},{7,4},{8,11},{9,10},{10,... | collective-permute-start | bytes 393224 | tf_op jit(solution)/shard_map/ppermute | solution.py:714
  14.5 65.4 %collective-permute-start.3 = (bf16[256,512]{1,0:T(8,128)(2,1)S(1)}, bf16[256,512]{1,0:T(8,128)(2,1)S(1)}, u32[]{:S(2)}, u32[]{:S(2)}) collective-permute-start(bf16[256,512]{1,0:T(8,128)(2,1)S(1)} %get-tuple-element.112), channel_id=1, source_target_pairs={{0,1},{1,0},{2,3},{3,2},{4,6},{5,7},{6,4},{7,5},{8,9},{9,8},{10,11... | collective-permute-start | bytes 786440 | tf_op jit(solution)/shard_map/ppermute | solution.py:728
  76.5 14.2 %collective-permute-start.28 = (bf16[256,512]{1,0:T(8,128)(2,1)S(1)}, bf16[256,512]{1,0:T(8,128)(2,1)S(1)}, u32[]{:S(2)}, u32[]{:S(2)}) collective-permute-start(bf16[256,512]{1,0:T(8,128)(2,1)S(1)} %get-tuple-element.128), channel_id=1, source_target_pairs={{0,2},{1,3},{2,0},{3,1},{4,5},{5,4},{6,7},{7,6},{8,10},{9,11},{10,... | collective-permute-start | bytes 786440 | tf_op jit(solution)/shard_map/ppermute | solution.py:728
  79.9 16.4 %collective-permute-start.37 = (bf16[256,512]{1,0:T(8,128)(2,1)S(1)}, bf16[256,512]{1,0:T(8,128)(2,1)S(1)}, u32[]{:S(2)}, u32[]{:S(2)}) collective-permute-start(bf16[256,512]{1,0:T(8,128)(2,1)S(1)} %get-tuple-element.134), channel_id=1, source_target_pairs={{0,2},{1,3},{2,0},{3,1},{4,5},{5,4},{6,7},{7,6},{8,10},{9,11},{10,... | collective-permute-start | bytes 786440 | tf_op jit(solution)/shard_map/ppermute | solution.py:728
  85.1 19.3 %collective-permute-start.18 = (bf16[2,256,512]{2,1,0:T(8,128)(2,1)}, bf16[2,256,512]{2,1,0:T(8,128)(2,1)S(1)}, u32[]{:S(2)}, u32[]{:S(2)}) collective-permute-start(bf16[2,256,512]{2,1,0:T(8,128)(2,1)} %get-tuple-element.121), channel_id=1, source_target_pairs={{0,1},{1,0},{2,3},{3,2},{4,6},{5,7},{6,4},{7,5},{8,9},{9,8},{10,11... | collective-permute-start | bytes 1572872 | tf_op jit(solution)/shard_map/ppermute | solution.py:728
  85.6 16.5 %collective-permute-start.36 = (bf16[256,512]{1,0:T(8,128)(2,1)S(1)}, bf16[256,512]{1,0:T(8,128)(2,1)S(1)}, u32[]{:S(2)}, u32[]{:S(2)}) collective-permute-start(bf16[256,512]{1,0:T(8,128)(2,1)S(1)} %get-tuple-element.134), channel_id=1, source_target_pairs={{0,1},{1,0},{2,3},{3,2},{4,6},{5,7},{6,4},{7,5},{8,9},{9,8},{10,11... | collective-permute-start | bytes 786440 | tf_op jit(solution)/shard_map/ppermute | solution.py:728
  103.6 18.1 %collective-permute-start.19 = (bf16[2,256,512]{2,1,0:T(8,128)(2,1)}, bf16[2,256,512]{2,1,0:T(8,128)(2,1)}, u32[]{:S(2)}, u32[]{:S(2)}) collective-permute-start(bf16[2,256,512]{2,1,0:T(8,128)(2,1)} %get-tuple-element.121), channel_id=1, source_target_pairs={{0,2},{1,3},{2,0},{3,1},{4,5},{5,4},{6,7},{7,6},{8,10},{9,11},{10,... | collective-permute-start | bytes 1572872 | tf_op jit(solution)/shard_map/ppermute | solution.py:728
  104.4 21.8 %collective-permute-start.20 = (bf16[2,256,512]{2,1,0:T(8,128)(2,1)S(1)}, bf16[2,256,512]{2,1,0:T(8,128)(2,1)}, u32[]{:S(2)}, u32[]{:S(2)}) collective-permute-start(bf16[2,256,512]{2,1,0:T(8,128)(2,1)S(1)} %collective-permute-done.18.rest_2_.rest_6_), channel_id=1, source_target_pairs={{0,2},{1,3},{2,0},{3,1},{4,5},{5,4},{6,7},{7,6},{8,10},{9,11},{10,... | collective-permute-start | bytes 1572872 | tf_op jit(solution)/shard_map/ppermute | solution.py:728
  121.6 37.2 %collective-permute-start.42 = (bf16[2,256,512]{2,1,0:T(8,128)(2,1)}, bf16[2,256,512]{2,1,0:T(8,128)(2,1)S(1)}, u32[]{:S(2)}, u32[]{:S(2)}) collective-permute-start(bf16[2,256,512]{2,1,0:T(8,128)(2,1)} %get-tuple-element.137), channel_id=1, source_target_pairs={{0,1},{1,0},{2,3},{3,2},{4,6},{5,7},{6,4},{7,5},{8,9},{9,8},{10,11... | collective-permute-start | bytes 1572872 | tf_op jit(solution)/shard_map/ppermute | solution.py:728
  122.2 36.6 %collective-permute-start.22 = (bf16[2,256,512]{2,1,0:T(8,128)(2,1)}, bf16[2,256,512]{2,1,0:T(8,128)(2,1)}, u32[]{:S(2)}, u32[]{:S(2)}) collective-permute-start(bf16[2,256,512]{2,1,0:T(8,128)(2,1)} %collective-permute-done.19.rest_3_.rest_7_), channel_id=1, source_target_pairs={{0,4},{4,0},{8,12},{12,8},{16,20},{20,16},{24,28},{28,24},{1,5},{5... | collective-permute-start | bytes 1572872 | tf_op jit(solution)/shard_map/ppermute | solution.py:710
  126.2 33.4 %collective-permute-start.21 = (bf16[2,256,512]{2,1,0:T(8,128)(2,1)S(1)}, bf16[2,256,512]{2,1,0:T(8,128)(2,1)}, u32[]{:S(2)}, u32[]{:S(2)}) collective-permute-start(bf16[2,256,512]{2,1,0:T(8,128)(2,1)S(1)} %collective-permute-done.18.rest_2_.rest_6_), channel_id=1, source_target_pairs={{0,4},{4,0},{8,12},{12,8},{16,20},{20,16},{24,28},{28,24},{1,5},{5... | collective-permute-start | bytes 1572872 | tf_op jit(solution)/shard_map/ppermute | solution.py:710
  126.2 33.5 %collective-permute-start.23 = (bf16[2,256,512]{2,1,0:T(8,128)(2,1)}, bf16[2,256,512]{2,1,0:T(8,128)(2,1)}, u32[]{:S(2)}, u32[]{:S(2)}) collective-permute-start(bf16[2,256,512]{2,1,0:T(8,128)(2,1)} %collective-permute-done.20.rest_4_.rest_8_), channel_id=1, source_target_pairs={{0,4},{4,0},{8,12},{12,8},{16,20},{20,16},{24,28},{28,24},{1,5},{5... | collective-permute-start | bytes 1572872 | tf_op jit(solution)/shard_map/ppermute | solution.py:710
  135.0 22.4 %collective-permute-start.29 = (bf16[256,512]{1,0:T(8,128)(2,1)S(1)}, bf16[256,512]{1,0:T(8,128)(2,1)S(1)}, u32[]{:S(2)}, u32[]{:S(2)}) collective-permute-start(bf16[256,512]{1,0:T(8,128)(2,1)S(1)} %collective-permute-done.27.rest_5_), channel_id=1, source_target_pairs={{0,2},{1,3},{2,0},{3,1},{4,5},{5,4},{6,7},{7,6},{8,10},{9,11},{10,... | collective-permute-start | bytes 786440 | tf_op jit(solution)/shard_map/ppermute | solution.py:728
  157.4 32.4 %collective-permute-start.43 = (bf16[2,256,512]{2,1,0:T(8,128)(2,1)}, bf16[2,256,512]{2,1,0:T(8,128)(2,1)S(1)}, u32[]{:S(2)}, u32[]{:S(2)}) collective-permute-start(bf16[2,256,512]{2,1,0:T(8,128)(2,1)} %get-tuple-element.137), channel_id=1, source_target_pairs={{0,2},{1,3},{2,0},{3,1},{4,5},{5,4},{6,7},{7,6},{8,10},{9,11},{10,... | collective-permute-start | bytes 1572872 | tf_op jit(solution)/shard_map/ppermute | solution.py:728
  159.7 30.6 %collective-permute-start.44 = (bf16[2,256,512]{2,1,0:T(8,128)(2,1)S(1)}, bf16[2,256,512]{2,1,0:T(8,128)(2,1)S(1)}, u32[]{:S(2)}, u32[]{:S(2)}) collective-permute-start(bf16[2,256,512]{2,1,0:T(8,128)(2,1)S(1)} %collective-permute-done.42.rest_2_), channel_id=1, source_target_pairs={{0,2},{1,3},{2,0},{3,1},{4,5},{5,4},{6,7},{7,6},{8,10},{9,11},{10,... | collective-permute-start | bytes 1572872 | tf_op jit(solution)/shard_map/ppermute | solution.py:728
  189.8 28.2 %collective-permute-start.45 = (bf16[2,256,512]{2,1,0:T(8,128)(2,1)S(1)}, bf16[2,256,512]{2,1,0:T(8,128)(2,1)S(1)}, u32[]{:S(2)}, u32[]{:S(2)}) collective-permute-start(bf16[2,256,512]{2,1,0:T(8,128)(2,1)S(1)} %collective-permute-done.42.rest_2_), channel_id=1, source_target_pairs={{0,4},{4,0},{8,12},{12,8},{16,20},{20,16},{24,28},{28,24},{1,5},{5... | collective-permute-start | bytes 1572872 | tf_op jit(solution)/shard_map/ppermute | solution.py:710
  189.8 28.2 %collective-permute-start.46 = (bf16[2,256,512]{2,1,0:T(8,128)(2,1)S(1)}, bf16[2,256,512]{2,1,0:T(8,128)(2,1)S(1)}, u32[]{:S(2)}, u32[]{:S(2)}) collective-permute-start(bf16[2,256,512]{2,1,0:T(8,128)(2,1)S(1)} %collective-permute-done.43.rest_3_), channel_id=1, source_target_pairs={{0,4},{4,0},{8,12},{12,8},{16,20},{20,16},{24,28},{28,24},{1,5},{5... | collective-permute-start | bytes 1572872 | tf_op jit(solution)/shard_map/ppermute | solution.py:710
  190.3 27.7 %collective-permute-start.47 = (bf16[2,256,512]{2,1,0:T(8,128)(2,1)S(1)}, bf16[2,256,512]{2,1,0:T(8,128)(2,1)S(1)}, u32[]{:S(2)}, u32[]{:S(2)}) collective-permute-start(bf16[2,256,512]{2,1,0:T(8,128)(2,1)S(1)} %collective-permute-done.44.rest_4_), channel_id=1, source_target_pairs={{0,4},{4,0},{8,12},{12,8},{16,20},{20,16},{24,28},{28,24},{1,5},{5... | collective-permute-start | bytes 1572872 | tf_op jit(solution)/shard_map/ppermute | solution.py:710
  352.0 33.2 %collective-permute-start.85 = (bf16[4,4,1,64,512]{4,3,2,1,0:T(8,128)(2,1)}, bf16[4,4,1,64,512]{4,3,2,1,0:T(8,128)(2,1)S(1)}, u32[]{:S(2)}, u32[]{:S(2)}) collective-permute-start(bf16[4,4,1,64,512]{4,3,2,1,0:T(8,128)(2,1)} %get-tuple-element.197), channel_id=1, source_target_pairs={{0,4},{4,0},{8,12},{12,8},{16,20},{20,16},{24,28},{28,24},{1,5},{5... | collective-permute-start | bytes 3145736 | tf_op jit(solution)/shard_map/ppermute | solution.py:710
  352.0 83.7 %collective-permute-start.95 = (bf16[4,4,2,64,512]{4,3,2,1,0:T(8,128)(2,1)}, bf16[4,4,2,64,512]{4,3,2,1,0:T(8,128)(2,1)}, u32[]{:S(2)}, u32[]{:S(2)}) collective-permute-start(bf16[4,4,2,64,512]{4,3,2,1,0:T(8,128)(2,1)} %get-tuple-element.201), channel_id=1, source_target_pairs={{0,4},{4,0},{8,12},{12,8},{16,20},{20,16},{24,28},{28,24},{1,5},{5... | collective-permute-start | bytes 6291464 | tf_op jit(solution)/shard_map/ppermute | solution.py:710
  359.6 26.4 %collective-permute-start.75 = (bf16[4,4,1,64,512]{4,3,2,1,0:T(8,128)(2,1)}, bf16[4,4,1,64,512]{4,3,2,1,0:T(8,128)(2,1)S(1)}, u32[]{:S(2)}, u32[]{:S(2)}) collective-permute-start(bf16[4,4,1,64,512]{4,3,2,1,0:T(8,128)(2,1)} %get-tuple-element.185), channel_id=1, source_target_pairs={{0,4},{4,0},{8,12},{12,8},{16,20},{20,16},{24,28},{28,24},{1,5},{5... | collective-permute-start | bytes 3145736 | tf_op jit(solution)/shard_map/ppermute | solution.py:710
  385.3 66.6 %collective-permute-start.90 = (bf16[4,4,2,64,512]{4,3,2,1,0:T(8,128)(2,1)}, bf16[4,4,2,64,512]{4,3,2,1,0:T(8,128)(2,1)}, u32[]{:S(2)}, u32[]{:S(2)}) collective-permute-start(bf16[4,4,2,64,512]{4,3,2,1,0:T(8,128)(2,1)} %get-tuple-element.199), channel_id=1, source_target_pairs={{0,4},{4,0},{8,12},{12,8},{16,20},{20,16},{24,28},{28,24},{1,5},{5... | collective-permute-start | bytes 6291464 | tf_op jit(solution)/shard_map/ppermute | solution.py:710
  388.5 20.8 %collective-permute-start.81 = (bf16[2,4,1,64,512]{4,3,1,2,0:T(8,128)(2,1)S(1)}, bf16[2,4,1,64,512]{4,3,1,2,0:T(8,128)(2,1)S(1)}, u32[]{:S(2)}, u32[]{:S(2)}) collective-permute-start(bf16[2,4,1,64,512]{4,3,1,2,0:T(8,128)(2,1)S(1)} %add_convert_fusion.5), channel_id=1, source_target_pairs={{0,2},{1,3},{2,0},{3,1},{4,5},{5,4},{6,7},{7,6},{8,10},{9,11},{10,... | collective-permute-start | bytes 1572872 | tf_op jit(solution)/shard_map/ppermute | solution.py:728
  395.2 28.4 %collective-permute-start.71 = (bf16[2,4,1,64,512]{4,3,1,2,0:T(8,128)(2,1)S(1)}, bf16[2,4,1,64,512]{4,3,1,2,0:T(8,128)(2,1)S(1)}, u32[]{:S(2)}, u32[]{:S(2)}) collective-permute-start(bf16[2,4,1,64,512]{4,3,1,2,0:T(8,128)(2,1)S(1)} %add_convert_fusion.7), channel_id=1, source_target_pairs={{0,2},{1,3},{2,0},{3,1},{4,5},{5,4},{6,7},{7,6},{8,10},{9,11},{10,... | collective-permute-start | bytes 1572872 | tf_op jit(solution)/shard_map/ppermute | solution.py:728
  411.4 22.0 %collective-permute-start.82 = (bf16[4,1,64,512]{3,2,1,0:T(8,128)(2,1)}, bf16[4,1,64,512]{3,2,1,0:T(8,128)(2,1)}, u32[]{:S(2)}, u32[]{:S(2)}) collective-permute-start(bf16[4,1,64,512]{3,2,1,0:T(8,128)(2,1)} %fusion.5), channel_id=1, source_target_pairs={{0,1},{1,0},{2,3},{3,2},{4,6},{5,7},{6,4},{7,5},{8,9},{9,8},{10,11... | collective-permute-start | bytes 786440 | tf_op jit(solution)/shard_map/ppermute | solution.py:728
  428.4 13.8 %collective-permute-start.72 = (bf16[4,1,64,512]{3,2,1,0:T(8,128)(2,1)}, bf16[4,1,64,512]{3,2,1,0:T(8,128)(2,1)}, u32[]{:S(2)}, u32[]{:S(2)}) collective-permute-start(bf16[4,1,64,512]{3,2,1,0:T(8,128)(2,1)} %fusion.4), channel_id=1, source_target_pairs={{0,1},{1,0},{2,3},{3,2},{4,6},{5,7},{6,4},{7,5},{8,9},{9,8},{10,11... | collective-permute-start | bytes 786440 | tf_op jit(solution)/shard_map/ppermute | solution.py:728
  438.5 17.0 %collective-permute-start.96 = (bf16[2,4,2,64,512]{4,3,2,1,0:T(8,128)(2,1)}, bf16[2,4,2,64,512]{4,3,2,1,0:T(8,128)(2,1)}, u32[]{:S(2)}, u32[]{:S(2)}) collective-permute-start(bf16[2,4,2,64,512]{4,3,2,1,0:T(8,128)(2,1)} %add_convert_fusion), channel_id=1, source_target_pairs={{0,2},{1,3},{2,0},{3,1},{4,5},{5,4},{6,7},{7,6},{8,10},{9,11},{10,... | collective-permute-start | bytes 3145736 | tf_op jit(solution)/shard_map/ppermute | solution.py:728
  453.8 18.6 %collective-permute-start.91 = (bf16[2,4,2,64,512]{4,3,2,1,0:T(8,128)(2,1)S(1)}, bf16[2,4,2,64,512]{4,3,2,1,0:T(8,128)(2,1)}, u32[]{:S(2)}, u32[]{:S(2)}) collective-permute-start(bf16[2,4,2,64,512]{4,3,2,1,0:T(8,128)(2,1)S(1)} %add_convert_fusion.1), channel_id=1, source_target_pairs={{0,2},{1,3},{2,0},{3,1},{4,5},{5,4},{6,7},{7,6},{8,10},{9,11},{10,... | collective-permute-start | bytes 3145736 | tf_op jit(solution)/shard_map/ppermute | solution.py:728
  484.5 15.2 %collective-permute-start.93 = (bf16[2,2,64,512]{3,2,1,0:T(8,128)(2,1)S(1)}, bf16[2,2,64,512]{3,2,1,0:T(8,128)(2,1)S(1)}, u32[]{:S(2)}, u32[]{:S(2)}) collective-permute-start(bf16[2,2,64,512]{3,2,1,0:T(8,128)(2,1)S(1)} %slice.674), channel_id=1, source_target_pairs={{0,16},{4,20},{8,24},{12,28},{16,0},{20,4},{24,8},{28,12},{1,17},{... | collective-permute-start | bytes 786440 | tf_op jit(solution)/shard_map/ppermute | solution.py:718
  (145 other events, 1488.5 us)
